TPU v7x, 32 devices: a whole 2x2x4 slice. The times are simulated.
32 devices in a mesh: gx: 4 (over y, core), gy: 2 (over x), gz: 4 (over z).
Axes of the slice: x: 2, y: 2, z: 4, core: 2. Of those that a mesh axis runs over, the one named last changes fastest.
Arguments:
- populations: float32 [19, 16, 16, 512], P(None, 'gz', 'gy', 'gx'), as said below
- porosity: float32 [16, 16, 512], P('gz', 'gy', 'gx'), may hold values from 0 to 1
- node_type: int32 [16, 16, 512], P('gz', 'gy', 'gx'), may hold values from 0 to 3, as said below
- step_index: int32 [1], replicated, may hold values from 0 to 4095
- adjoint_end: float32 [19, 16, 16, 512], P(None, 'gz', 'gy', 'gx'), may hold values from -6 to 6
Outputs:
- adjoint_start: float32 [19, 16, 16, 512], P(None, 'gz', 'gy', 'gx')
- sensitivity: float32 [16, 16, 512], P('gz', 'gy', 'gx')
Inputs may be any that keep to these rules, and one draw needn't show every extreme that they name: `populations`: every entry is positive, between 0.4 and 1.9 times its velocity's weight. `node_type`: cells of the first and last planes across the span and along the depth are walls, as are scattered obstacle cells; the other cells of the first plane along the stream are inlets, of the last plane outlets.
All inputs are finite; a program needn't handle non-finite values.
Results may differ from a plain program's by a relative error of at most 0.0001.
Values sent between devices are 32-bit elements; how exact they have to be, the bound alone decides.
A program may use at most 64 MiB of HBM per device.

v0:
```python
import math

import jax
import jax.numpy as jnp
from jax import lax
from jax.sharding import PartitionSpec as P

STEPS = 2


lattice_velocities = (
    (0, 0, 0),
    (1, 0, 0),
    (-1, 0, 0),
    (0, 1, 0),
    (0, -1, 0),
    (0, 0, 1),
    (0, 0, -1),
    (1, 1, 0),
    (-1, -1, 0),
    (1, -1, 0),
    (-1, 1, 0),
    (1, 0, 1),
    (-1, 0, -1),
    (1, 0, -1),
    (-1, 0, 1),
    (0, 1, 1),
    (0, -1, -1),
    (0, 1, -1),
    (0, -1, 1),
)
lattice_weights = (1.0 / 3.0,) + (1.0 / 18.0,) * 6 + (1.0 / 36.0,) * 12
opposite_index = (0, 2, 1, 4, 3, 6, 5, 8, 7, 10, 9, 12, 11, 14, 13, 16, 15, 18, 17)
relax_rate = 1.25
ramp_factor = 0.1
inlet_base = 0.1
inlet_period = 64.0


def with_halo(block, sides, width):
    for axis, dim in sides:
        count = lax.axis_size(axis)
        forward = [(i, i + 1) for i in range(count - 1)]
        forward.append((count - 1, 0))
        backward = [(target, source) for source, target in forward]
        low = lax.ppermute(
            lax.slice_in_dim(block, block.shape[dim] - width, None, axis=dim), axis, forward
        )
        high = lax.ppermute(lax.slice_in_dim(block, 0, width, axis=dim), axis, backward)
        block = jnp.concatenate([low, block, high], axis=dim)
    return block


def lattice_column(which):
    return jnp.asarray([vector[which] for vector in lattice_velocities], jnp.float32)[
        :, None, None, None
    ]


def weight_column():
    return jnp.asarray(lattice_weights, jnp.float32)[:, None, None, None]


def equilibrium(density, flow_east, flow_north, flow_depth):
    projected = (
        lattice_column(0) * flow_east
        + lattice_column(1) * flow_north
        + lattice_column(2) * flow_depth
    )
    square = flow_east * flow_east + flow_north * flow_north + flow_depth * flow_depth
    return (
        weight_column()
        * density
        * (1.0 + 3.0 * projected + 4.5 * projected * projected - 1.5 * square)
    )


def collide(current, porosity, node_kinds, inlet_speed):
    density = jnp.sum(current, axis=0)
    flow_east = jnp.sum(lattice_column(0) * current, axis=0) / density
    flow_north = jnp.sum(lattice_column(1) * current, axis=0) / density
    flow_depth = jnp.sum(lattice_column(2) * current, axis=0) / density
    damping = ramp_factor * (1.0 - porosity) / (ramp_factor + porosity)
    retained = 1.0 - damping
    relaxed = current - relax_rate * (
        current
        - equilibrium(density, retained * flow_east, retained * flow_north, retained * flow_depth)
    )
    bounced = current[jnp.asarray(opposite_index)]
    unit_field = jnp.ones_like(density)
    inflow = equilibrium(unit_field, inlet_speed * unit_field, 0.0 * unit_field, 0.0 * unit_field)
    outflow = equilibrium(density, flow_east, flow_north, flow_depth)
    collided = jnp.where(
        node_kinds == 1,
        bounced,
        jnp.where(node_kinds == 2, inflow, jnp.where(node_kinds == 3, outflow, relaxed)),
    )
    kinetic = flow_east * flow_east + flow_north * flow_north + flow_depth * flow_depth
    energy = jnp.where(node_kinds == 0, damping * density * kinetic, 0.0 * density)
    return (collided, energy)


def inlet_value(step_index, offset):
    moment = (step_index[0] + offset).astype(jnp.float32)
    return inlet_base * (1.0 + 0.8 * jnp.sin(2.0 * math.pi * moment / inlet_period))


def trim_pull(padded, sign):
    extent_z, extent_y, extent_x = padded.shape[1:]
    slabs = []
    for q in range(len(lattice_velocities)):
        vector = lattice_velocities[q]
        move_east = sign * vector[0]
        move_north = sign * vector[1]
        move_depth = sign * vector[2]
        slabs.append(
            padded[
                q,
                1 - move_depth : extent_z - 1 - move_depth,
                1 - move_north : extent_y - 1 - move_north,
                1 - move_east : extent_x - 1 - move_east,
            ]
        )
    return jnp.stack(slabs)


def stream_field(field, sign):
    padded = with_halo(field, (("gx", 3), ("gy", 2), ("gz", 1)), 1)
    return trim_pull(padded, sign)


def on_device(populations, porosity, node_type, step_index, adjoint_end):
    states = []
    current = populations
    for t in range(STEPS):
        states.append(current)
        if t + 1 < STEPS:
            collided, energy = collide(current, porosity, node_type, inlet_value(step_index, t))
            current = stream_field(collided, 1)
    adjoint = adjoint_end
    sensitivity = jnp.zeros_like(porosity)
    for t in reversed(range(STEPS)):
        arriving = stream_field(adjoint, -1)
        inlet_speed = inlet_value(step_index, t)

        def local_step(incoming, design, inlet_speed=inlet_speed):
            return collide(incoming, design, node_type, inlet_speed)

        collided, pullback = jax.vjp(local_step, states[t], porosity)
        adjoint, design_grad = pullback((arriving, jnp.ones_like(porosity)))
        sensitivity = sensitivity + design_grad
    return (adjoint, sensitivity)


def solution(mesh):
    return jax.shard_map(
        on_device,
        mesh=mesh,
        in_specs=(
            P(None, "gz", "gy", "gx"),
            P("gz", "gy", "gx"),
            P("gz", "gy", "gx"),
            P(),
            P(None, "gz", "gy", "gx"),
        ),
        out_specs=(P(None, "gz", "gy", "gx"), P("gz", "gy", "gx")),
        check_vma=False,
    )
```

profile of v0, /device:TPU:0, one launch (start us, length us, event | category | flops | bytes accessed | tf_op | source)
XLA Modules:
  0.0 100.9 jit_solution(9082969186089386100)
XLA Ops:
  0.6 0.7 broadcast_compare_fusion.3
  2.1 0.6 copy-done.9
  2.8 1.6 %gather_fusion = f32[19,4,8,128]{3,2,1,0:T(8,128)S(1)} fusion(f32[19,4,8,128]{3,2,1,0:T(8,128)} %param.45, s32[1024]{0:T(1024)S(1)} %pad_clamp_fusion), kind=kCustom, calls=%fused_computation | custom fusion | bytes 622668 | tf_op jit(solution)/shard_map/gather | solution.py:89
  4.4 0.1 multiply_reduce_fusion.17
  4.6 0.7 copy-done.3
  5.3 0.6 copy-done.8
  6.0 0.5 fusion.24
  6.5 0.2 fusion.57
  6.7 0.5 collective-permute-start.6
  7.2 2.0 %collective-permute-start.7 = (f32[19,4,8,1]{3,2,1,0:T(8,128)S(1)}, f32[19,4,8,1]{3,2,1,0:T(8,128)S(1)}, u32[]{:S(2)}, u32[]{:S(2)}) collective-permute-start(f32[19,4,8,1]{3,2,1,0:T(8,128)S(1)} %get-tuple-element.124), channel_id=1, source_target_pairs={{8,0},{16,8},{24,16},{0,24},{9,1},{17,9},{25,17},{1,25},{10,2},{18... | collective-permute-start | bytes 7304 | tf_op jit(solution)/shard_map/ppermute | solution.py:49
  9.2 0.2 fusion.58
  9.4 0.7 collective-permute-start
  10.1 4.3 %collective-permute-done.6 = f32[19,4,8,1]{3,2,1,0:T(8,128)S(1)} collective-permute-done((f32[19,4,8,1]{3,2,1,0:T(8,128)S(1)}, f32[19,4,8,1]{3,2,1,0:T(8,128)S(1)}, u32[]{:S(2)}, u32[]{:S(2)}) %collective-permute-start.6) | collective-permute-done | bytes 2464 | tf_op jit(solution)/shard_map/ppermute | solution.py:46
  14.4 2.6 %collective-permute-done.7 = f32[19,4,8,1]{3,2,1,0:T(8,128)S(1)} collective-permute-done((f32[19,4,8,1]{3,2,1,0:T(8,128)S(1)}, f32[19,4,8,1]{3,2,1,0:T(8,128)S(1)}, u32[]{:S(2)}, u32[]{:S(2)}) %collective-permute-start.7) | collective-permute-done | bytes 2464 | tf_op jit(solution)/shard_map/ppermute | solution.py:49
  17.0 0.5 pad_maximum_fusion.18
  17.5 2.3 %collective-permute-start.8 = (f32[19,4,1,130]{3,2,1,0:T(1,128)S(1)}, f32[19,4,1,130]{3,2,1,0:T(1,128)S(1)}, u32[]{:S(2)}, u32[]{:S(2)}) collective-permute-start(f32[19,4,1,130]{3,2,1,0:T(1,128)S(1)} %get-tuple-element.112), channel_id=1, source_target_pairs={{0,4},{4,0},{1,5},{5,1},{2,6},{6,2},{3,7},{7,3},{8,12},{12,8},{9,1... | collective-permute-start | bytes 118568 | tf_op jit(solution)/shard_map/ppermute | solution.py:46
  19.9 3.7 %collective-permute-done = f32[19,4,8,1]{3,2,1,0:T(8,128)S(1)} collective-permute-done((f32[19,4,8,1]{3,2,1,0:T(8,128)S(1)}, f32[19,4,8,1]{3,2,1,0:T(8,128)S(1)}, u32[]{:S(2)}, u32[]{:S(2)}) %collective-permute-start) | collective-permute-done | bytes 2464 | tf_op jit(solution)/shard_map/ppermute | solution.py:49
  23.6 0.5 pad_maximum_fusion.21
  24.1 1.6 %collective-permute-start.2 = (f32[19,4,1,130]{3,2,1,0:T(1,128)S(1)}, f32[19,4,1,130]{3,2,1,0:T(1,128)S(1)}, u32[]{:S(2)}, u32[]{:S(2)}) collective-permute-start(f32[19,4,1,130]{3,2,1,0:T(1,128)S(1)} %get-tuple-element.114), channel_id=1, source_target_pairs={{4,0},{0,4},{5,1},{1,5},{6,2},{2,6},{7,3},{3,7},{12,8},{8,12},{13,... | collective-permute-start | bytes 118568 | tf_op jit(solution)/shard_map/ppermute | solution.py:49
  25.7 0.5 collective-permute-start.3
  26.5 0.3 pad_maximum_fusion.5
  26.8 1.6 %collective-permute-start.10 = (f32[19,1,10,130]{3,2,1,0:T(8,128)S(1)}, f32[19,1,10,130]{3,2,1,0:T(8,128)S(1)}, u32[]{:S(2)}, u32[]{:S(2)}) collective-permute-start(f32[19,1,10,130]{3,2,1,0:T(8,128)S(1)} %get-tuple-element.106), channel_id=1, source_target_pairs={{0,1},{1,2},{2,3},{3,0},{4,5},{5,6},{6,7},{7,4},{8,9},{9,10},{10,1... | collective-permute-start | bytes 296408 | tf_op jit(solution)/shard_map/ppermute | solution.py:46
  28.5 2.3 %collective-permute-start.11 = (f32[19,1,10,130]{3,2,1,0:T(8,128)S(1)}, f32[19,1,10,130]{3,2,1,0:T(8,128)S(1)}, u32[]{:S(2)}, u32[]{:S(2)}) collective-permute-start(f32[19,1,10,130]{3,2,1,0:T(8,128)S(1)} %get-tuple-element.105), channel_id=1, source_target_pairs={{1,0},{2,1},{3,2},{0,3},{5,4},{6,5},{7,6},{4,7},{9,8},{10,9},{11,1... | collective-permute-start | bytes 296408 | tf_op jit(solution)/shard_map/ppermute | solution.py:49
  30.7 0.3 pad_maximum_fusion.10
  31.1 3.9 %collective-permute-start.4 = (f32[19,1,10,130]{3,2,1,0:T(8,128)S(1)}, f32[19,1,10,130]{3,2,1,0:T(8,128)S(1)}, u32[]{:S(2)}, u32[]{:S(2)}) collective-permute-start(f32[19,1,10,130]{3,2,1,0:T(8,128)S(1)} %get-tuple-element.108), channel_id=1, source_target_pairs={{1,0},{2,1},{3,2},{0,3},{5,4},{6,5},{7,6},{4,7},{9,8},{10,9},{11,1... | collective-permute-start | bytes 296408 | tf_op jit(solution)/shard_map/ppermute | solution.py:49
  35.3 3.6 %collective-permute-done.10 = f32[19,1,10,130]{3,2,1,0:T(8,128)S(1)} collective-permute-done((f32[19,1,10,130]{3,2,1,0:T(8,128)S(1)}, f32[19,1,10,130]{3,2,1,0:T(8,128)S(1)}, u32[]{:S(2)}, u32[]{:S(2)}) %collective-permute-start.10) | collective-permute-done | bytes 98832 | tf_op jit(solution)/shard_map/ppermute | solution.py:46
  39.0 6.3 %collective-permute-done.11 = f32[19,1,10,130]{3,2,1,0:T(8,128)S(1)} collective-permute-done((f32[19,1,10,130]{3,2,1,0:T(8,128)S(1)}, f32[19,1,10,130]{3,2,1,0:T(8,128)S(1)}, u32[]{:S(2)}, u32[]{:S(2)}) %collective-permute-start.11) | collective-permute-done | bytes 98832 | tf_op jit(solution)/shard_map/ppermute | solution.py:49
  45.7 0.1 constant_dynamic-update-slice_fusion.26
  46.1 0.1 constant_dynamic-update-slice_fusion.21
  46.2 0.1 constant_dynamic-update-slice_fusion.19
  46.3 0.1 multiply_reduce_fusion.16
  46.6 4.7 %collective-permute-done.4 = f32[19,1,10,130]{3,2,1,0:T(8,128)S(1)} collective-permute-done((f32[19,1,10,130]{3,2,1,0:T(8,128)S(1)}, f32[19,1,10,130]{3,2,1,0:T(8,128)S(1)}, u32[]{:S(2)}, u32[]{:S(2)}) %collective-permute-start.4) | collective-permute-done | bytes 98832 | tf_op jit(solution)/shard_map/ppermute | solution.py:49
  51.4 7.2 %collective-permute-done.5 = f32[19,1,10,130]{3,2,1,0:T(8,128)S(1)} collective-permute-done((f32[19,1,10,130]{3,2,1,0:T(8,128)S(1)}, f32[19,1,10,130]{3,2,1,0:T(8,128)S(1)}, u32[]{:S(2)}, u32[]{:S(2)}) %collective-permute-start.5) | collective-permute-done | bytes 98832 | tf_op jit(solution)/shard_map/ppermute | solution.py:46
  58.9 0.1 constant_dynamic-update-slice_fusion.8
  59.2 0.1 constant_dynamic-update-slice_fusion.4
  59.3 0.1 constant_dynamic-update-slice_fusion.3
  59.5 0.1 constant_dynamic-update-slice_fusion.1
  59.6 0.4 fusion.9
  60.1 0.6 fusion.30
  60.9 0.2 broadcast_select_fusion.1
  61.1 1.9 %scatter_fusion = f32[19,4,8,128]{3,2,1,0:T(8,128)S(1)} fusion(f32[19,4,8,128]{3,2,1,0:T(8,128)S(1)} %get-tuple-element.121, s32[19]{0:T(128)S(1)} %copy-done.9, f32[19,4,8,128]{3,2,1,0:T(8,128)S(1)} %get-tuple-element.120), kind=kCustom, calls=%fused_computation.1 | custom fusion | flops 77824 | bytes 933964 | tf_op jit(solution)/shard_map/transpose(jvp())/scatter-add | solution.py:89
  63.0 0.2 fusion.56
  63.2 0.5 collective-permute-start.13
  63.7 6.2 %collective-permute-done.12 = f32[19,4,8,1]{3,2,1,0:T(8,128)S(1)} collective-permute-done((f32[19,4,8,1]{3,2,1,0:T(8,128)S(1)}, f32[19,4,8,1]{3,2,1,0:T(8,128)S(1)}, u32[]{:S(2)}, u32[]{:S(2)}) %collective-permute-start.12) | collective-permute-done | bytes 2464 | tf_op jit(solution)/shard_map/ppermute | solution.py:49
  69.9 3.0 %collective-permute-done.13 = f32[19,4,8,1]{3,2,1,0:T(8,128)S(1)} collective-permute-done((f32[19,4,8,1]{3,2,1,0:T(8,128)S(1)}, f32[19,4,8,1]{3,2,1,0:T(8,128)S(1)}, u32[]{:S(2)}, u32[]{:S(2)}) %collective-permute-start.13) | collective-permute-done | bytes 2464 | tf_op jit(solution)/shard_map/ppermute | solution.py:46
  72.9 0.5 pad_maximum_fusion.15
  73.4 1.6 %collective-permute-start.14 = (f32[19,4,1,130]{3,2,1,0:T(1,128)S(1)}, f32[19,4,1,130]{3,2,1,0:T(1,128)S(1)}, u32[]{:S(2)}, u32[]{:S(2)}) collective-permute-start(f32[19,4,1,130]{3,2,1,0:T(1,128)S(1)} %get-tuple-element.110), channel_id=1, source_target_pairs={{4,0},{0,4},{5,1},{1,5},{6,2},{2,6},{7,3},{3,7},{12,8},{8,12},{13,... | collective-permute-start | bytes 118568 | tf_op jit(solution)/shard_map/ppermute | solution.py:49
  75.0 0.5 collective-permute-start.15
  75.7 3.0 %collective-permute-done.14 = f32[19,4,1,130]{3,2,1,0:T(1,128)S(1)} collective-permute-done((f32[19,4,1,130]{3,2,1,0:T(1,128)S(1)}, f32[19,4,1,130]{3,2,1,0:T(1,128)S(1)}, u32[]{:S(2)}, u32[]{:S(2)}) %collective-permute-start.14) | collective-permute-done | bytes 39552 | tf_op jit(solution)/shard_map/ppermute | solution.py:49
  78.7 0.8 collective-permute-done.15
  79.6 0.3 pad_maximum_fusion
  79.9 1.6 %collective-permute-start.16 = (f32[19,1,10,130]{3,2,1,0:T(8,128)S(1)}, f32[19,1,10,130]{3,2,1,0:T(8,128)S(1)}, u32[]{:S(2)}, u32[]{:S(2)}) collective-permute-start(f32[19,1,10,130]{3,2,1,0:T(8,128)S(1)} %get-tuple-element.104), channel_id=1, source_target_pairs={{1,0},{2,1},{3,2},{0,3},{5,4},{6,5},{7,6},{4,7},{9,8},{10,9},{11,1... | collective-permute-start | bytes 296408 | tf_op jit(solution)/shard_map/ppermute | solution.py:49
  81.5 0.5 collective-permute-start.17
  82.1 13.0 %collective-permute-done.16 = f32[19,1,10,130]{3,2,1,0:T(8,128)S(1)} collective-permute-done((f32[19,1,10,130]{3,2,1,0:T(8,128)S(1)}, f32[19,1,10,130]{3,2,1,0:T(8,128)S(1)}, u32[]{:S(2)}, u32[]{:S(2)}) %collective-permute-start.16) | collective-permute-done | bytes 98832 | tf_op jit(solution)/shard_map/ppermute | solution.py:49
  95.5 0.1 constant_dynamic-update-slice_fusion.46
  95.9 0.1 constant_dynamic-update-slice_fusion.42
  96.0 0.1 constant_dynamic-update-slice_fusion.41
  96.1 0.1 constant_dynamic-update-slice_fusion.39
  96.3 0.5 fusion.7
  96.7 0.6 fusion.31
  97.4 0.7 add_add_fusion.9
  98.1 0.1 add_add_fusion
  98.2 1.9 %scatter_fusion.1 = f32[19,4,8,128]{3,2,1,0:T(8,128)S(1)} fusion(f32[19,4,8,128]{3,2,1,0:T(8,128)S(1)} %add_add_fusion, s32[19]{0:T(128)S(1)} %copy-done.9, f32[19,4,8,128]{3,2,1,0:T(8,128)S(1)} %get-tuple-element.119), kind=kCustom, calls=%fused_computation.2 | custom fusion | flops 77824 | bytes 933964 | tf_op jit(solution)/shard_map/transpose(jvp())/scatter-add | solution.py:89
  100.2 0.7 copy-done.2
  (86 shorter events, 3.9 us)
Async XLA Ops:
  2.1 0.7 copy-start.9
  2.8 1.6 %copy-start.1 = (f32[19,4,8,128]{3,2,1,0:T(8,128)S(1)}, f32[19,4,8,128]{3,2,1,0:T(8,128)}, u32[]{:S(2)}) copy-start(f32[19,4,8,128]{3,2,1,0:T(8,128)} %param.45) | copy-start | bytes 933892
  2.8 1.6 %copy-start.5 = (f32[19]{0:T(128)S(1)}, f32[19]{0:T(128)}, u32[]{:S(2)}) copy-start(f32[19]{0:T(128)} %constant.63.clone) | copy-start | bytes 232
  2.8 1.6 %copy-start.6 = (f32[19]{0:T(128)S(1)}, f32[19]{0:T(128)}, u32[]{:S(2)}) copy-start(f32[19]{0:T(128)} %constant.64.clone) | copy-start | bytes 232
  2.8 1.6 %copy-start.7 = (f32[19]{0:T(128)S(1)}, f32[19]{0:T(128)}, u32[]{:S(2)}) copy-start(f32[19]{0:T(128)} %constant.65.clone) | copy-start | bytes 232
  4.5 0.7 copy-start.3
  5.3 0.7 copy-start.8
  5.3 0.7 copy-start.10
  6.5 2.7 %copy-start = (f32[19,4,8,128]{3,2,1,0:T(8,128)S(1)}, f32[19,4,8,128]{3,2,1,0:T(8,128)}, u32[]{:S(2)}) copy-start(f32[19,4,8,128]{3,2,1,0:T(8,128)} %param.49) | copy-start | bytes 933892
  6.7 7.7 %collective-permute-start.6 = (f32[19,4,8,1]{3,2,1,0:T(8,128)S(1)}, f32[19,4,8,1]{3,2,1,0:T(8,128)S(1)}, u32[]{:S(2)}, u32[]{:S(2)}) collective-permute-start(f32[19,4,8,1]{3,2,1,0:T(8,128)S(1)} %get-tuple-element.125), channel_id=1, source_target_pairs={{0,8},{8,16},{16,24},{24,0},{1,9},{9,17},{17,25},{25,1},{2,10},{10... | collective-permute-start | bytes 7304 | tf_op jit(solution)/shard_map/ppermute | solution.py:46
  7.2 9.8 %collective-permute-start.7 = (f32[19,4,8,1]{3,2,1,0:T(8,128)S(1)}, f32[19,4,8,1]{3,2,1,0:T(8,128)S(1)}, u32[]{:S(2)}, u32[]{:S(2)}) collective-permute-start(f32[19,4,8,1]{3,2,1,0:T(8,128)S(1)} %get-tuple-element.124), channel_id=1, source_target_pairs={{8,0},{16,8},{24,16},{0,24},{9,1},{17,9},{25,17},{1,25},{10,2},{18... | collective-permute-start | bytes 7304 | tf_op jit(solution)/shard_map/ppermute | solution.py:49
  9.4 14.2 %collective-permute-start = (f32[19,4,8,1]{3,2,1,0:T(8,128)S(1)}, f32[19,4,8,1]{3,2,1,0:T(8,128)S(1)}, u32[]{:S(2)}, u32[]{:S(2)}) collective-permute-start(f32[19,4,8,1]{3,2,1,0:T(8,128)S(1)} %get-tuple-element.127), channel_id=1, source_target_pairs={{8,0},{16,8},{24,16},{0,24},{9,1},{17,9},{25,17},{1,25},{10,2},{18... | collective-permute-start | bytes 7304 | tf_op jit(solution)/shard_map/ppermute | solution.py:49
  10.1 13.5 %collective-permute-start.1 = (f32[19,4,8,1]{3,2,1,0:T(8,128)S(1)}, f32[19,4,8,1]{3,2,1,0:T(8,128)S(1)}, u32[]{:S(2)}, u32[]{:S(2)}) collective-permute-start(f32[19,4,8,1]{3,2,1,0:T(8,128)S(1)} %get-tuple-element.126), channel_id=1, source_target_pairs={{0,8},{8,16},{16,24},{24,0},{1,9},{9,17},{17,25},{25,1},{2,10},{10... | collective-permute-start | bytes 7304 | tf_op jit(solution)/shard_map/ppermute | solution.py:46
  17.5 9.0 %collective-permute-start.8 = (f32[19,4,1,130]{3,2,1,0:T(1,128)S(1)}, f32[19,4,1,130]{3,2,1,0:T(1,128)S(1)}, u32[]{:S(2)}, u32[]{:S(2)}) collective-permute-start(f32[19,4,1,130]{3,2,1,0:T(1,128)S(1)} %get-tuple-element.112), channel_id=1, source_target_pairs={{0,4},{4,0},{1,5},{5,1},{2,6},{6,2},{3,7},{7,3},{8,12},{12,8},{9,1... | collective-permute-start | bytes 118568 | tf_op jit(solution)/shard_map/ppermute | solution.py:46
  19.8 6.7 %collective-permute-start.9 = (f32[19,4,1,130]{3,2,1,0:T(1,128)S(1)}, f32[19,4,1,130]{3,2,1,0:T(1,128)S(1)}, u32[]{:S(2)}, u32[]{:S(2)}) collective-permute-start(f32[19,4,1,130]{3,2,1,0:T(1,128)S(1)} %get-tuple-element.111), channel_id=1, source_target_pairs={{4,0},{0,4},{5,1},{1,5},{6,2},{2,6},{7,3},{3,7},{12,8},{8,12},{13,... | collective-permute-start | bytes 118568 | tf_op jit(solution)/shard_map/ppermute | solution.py:49
  24.1 6.6 %collective-permute-start.2 = (f32[19,4,1,130]{3,2,1,0:T(1,128)S(1)}, f32[19,4,1,130]{3,2,1,0:T(1,128)S(1)}, u32[]{:S(2)}, u32[]{:S(2)}) collective-permute-start(f32[19,4,1,130]{3,2,1,0:T(1,128)S(1)} %get-tuple-element.114), channel_id=1, source_target_pairs={{4,0},{0,4},{5,1},{1,5},{6,2},{2,6},{7,3},{3,7},{12,8},{8,12},{13,... | collective-permute-start | bytes 118568 | tf_op jit(solution)/shard_map/ppermute | solution.py:49
  25.7 5.1 %collective-permute-start.3 = (f32[19,4,1,130]{3,2,1,0:T(1,128)S(1)}, f32[19,4,1,130]{3,2,1,0:T(1,128)S(1)}, u32[]{:S(2)}, u32[]{:S(2)}) collective-permute-start(f32[19,4,1,130]{3,2,1,0:T(1,128)S(1)} %get-tuple-element.113), channel_id=1, source_target_pairs={{0,4},{4,0},{1,5},{5,1},{2,6},{6,2},{3,7},{7,3},{8,12},{12,8},{9,1... | collective-permute-start | bytes 118568 | tf_op jit(solution)/shard_map/ppermute | solution.py:46
  26.8 12.0 %collective-permute-start.10 = (f32[19,1,10,130]{3,2,1,0:T(8,128)S(1)}, f32[19,1,10,130]{3,2,1,0:T(8,128)S(1)}, u32[]{:S(2)}, u32[]{:S(2)}) collective-permute-start(f32[19,1,10,130]{3,2,1,0:T(8,128)S(1)} %get-tuple-element.106), channel_id=1, source_target_pairs={{0,1},{1,2},{2,3},{3,0},{4,5},{5,6},{6,7},{7,4},{8,9},{9,10},{10,1... | collective-permute-start | bytes 296408 | tf_op jit(solution)/shard_map/ppermute | solution.py:46
  28.5 16.8 %collective-permute-start.11 = (f32[19,1,10,130]{3,2,1,0:T(8,128)S(1)}, f32[19,1,10,130]{3,2,1,0:T(8,128)S(1)}, u32[]{:S(2)}, u32[]{:S(2)}) collective-permute-start(f32[19,1,10,130]{3,2,1,0:T(8,128)S(1)} %get-tuple-element.105), channel_id=1, source_target_pairs={{1,0},{2,1},{3,2},{0,3},{5,4},{6,5},{7,6},{4,7},{9,8},{10,9},{11,1... | collective-permute-start | bytes 296408 | tf_op jit(solution)/shard_map/ppermute | solution.py:49
  31.1 20.3 %collective-permute-start.4 = (f32[19,1,10,130]{3,2,1,0:T(8,128)S(1)}, f32[19,1,10,130]{3,2,1,0:T(8,128)S(1)}, u32[]{:S(2)}, u32[]{:S(2)}) collective-permute-start(f32[19,1,10,130]{3,2,1,0:T(8,128)S(1)} %get-tuple-element.108), channel_id=1, source_target_pairs={{1,0},{2,1},{3,2},{0,3},{5,4},{6,5},{7,6},{4,7},{9,8},{10,9},{11,1... | collective-permute-start | bytes 296408 | tf_op jit(solution)/shard_map/ppermute | solution.py:49
  34.9 23.7 %collective-permute-start.5 = (f32[19,1,10,130]{3,2,1,0:T(8,128)S(1)}, f32[19,1,10,130]{3,2,1,0:T(8,128)S(1)}, u32[]{:S(2)}, u32[]{:S(2)}) collective-permute-start(f32[19,1,10,130]{3,2,1,0:T(8,128)S(1)} %get-tuple-element.107), channel_id=1, source_target_pairs={{0,1},{1,2},{2,3},{3,0},{4,5},{5,6},{6,7},{7,4},{8,9},{9,10},{10,1... | collective-permute-start | bytes 296408 | tf_op jit(solution)/shard_map/ppermute | solution.py:46
  60.1 0.7 copy-start.4
  63.1 6.8 %collective-permute-start.12 = (f32[19,4,8,1]{3,2,1,0:T(8,128)S(1)}, f32[19,4,8,1]{3,2,1,0:T(8,128)S(1)}, u32[]{:S(2)}, u32[]{:S(2)}) collective-permute-start(f32[19,4,8,1]{3,2,1,0:T(8,128)S(1)} %get-tuple-element.123), channel_id=1, source_target_pairs={{8,0},{16,8},{24,16},{0,24},{9,1},{17,9},{25,17},{1,25},{10,2},{18... | collective-permute-start | bytes 7304 | tf_op jit(solution)/shard_map/ppermute | solution.py:49
  63.2 9.7 %collective-permute-start.13 = (f32[19,4,8,1]{3,2,1,0:T(8,128)S(1)}, f32[19,4,8,1]{3,2,1,0:T(8,128)S(1)}, u32[]{:S(2)}, u32[]{:S(2)}) collective-permute-start(f32[19,4,8,1]{3,2,1,0:T(8,128)S(1)} %get-tuple-element.122), channel_id=1, source_target_pairs={{0,8},{8,16},{16,24},{24,0},{1,9},{9,17},{17,25},{25,1},{2,10},{10... | collective-permute-start | bytes 7304 | tf_op jit(solution)/shard_map/ppermute | solution.py:46
  73.4 5.3 %collective-permute-start.14 = (f32[19,4,1,130]{3,2,1,0:T(1,128)S(1)}, f32[19,4,1,130]{3,2,1,0:T(1,128)S(1)}, u32[]{:S(2)}, u32[]{:S(2)}) collective-permute-start(f32[19,4,1,130]{3,2,1,0:T(1,128)S(1)} %get-tuple-element.110), channel_id=1, source_target_pairs={{4,0},{0,4},{5,1},{1,5},{6,2},{2,6},{7,3},{3,7},{12,8},{8,12},{13,... | collective-permute-start | bytes 118568 | tf_op jit(solution)/shard_map/ppermute | solution.py:49
  75.0 4.5 %collective-permute-start.15 = (f32[19,4,1,130]{3,2,1,0:T(1,128)S(1)}, f32[19,4,1,130]{3,2,1,0:T(1,128)S(1)}, u32[]{:S(2)}, u32[]{:S(2)}) collective-permute-start(f32[19,4,1,130]{3,2,1,0:T(1,128)S(1)} %get-tuple-element.109), channel_id=1, source_target_pairs={{0,4},{4,0},{1,5},{5,1},{2,6},{6,2},{3,7},{7,3},{8,12},{12,8},{9,1... | collective-permute-start | bytes 118568 | tf_op jit(solution)/shard_map/ppermute | solution.py:46
  79.9 15.3 %collective-permute-start.16 = (f32[19,1,10,130]{3,2,1,0:T(8,128)S(1)}, f32[19,1,10,130]{3,2,1,0:T(8,128)S(1)}, u32[]{:S(2)}, u32[]{:S(2)}) collective-permute-start(f32[19,1,10,130]{3,2,1,0:T(8,128)S(1)} %get-tuple-element.104), channel_id=1, source_target_pairs={{1,0},{2,1},{3,2},{0,3},{5,4},{6,5},{7,6},{4,7},{9,8},{10,9},{11,1... | collective-permute-start | bytes 296408 | tf_op jit(solution)/shard_map/ppermute | solution.py:49
  81.5 13.7 %collective-permute-start.17 = (f32[19,1,10,130]{3,2,1,0:T(8,128)S(1)}, f32[19,1,10,130]{3,2,1,0:T(8,128)S(1)}, u32[]{:S(2)}, u32[]{:S(2)}) collective-permute-start(f32[19,1,10,130]{3,2,1,0:T(8,128)S(1)} %get-tuple-element.103), channel_id=1, source_target_pairs={{0,1},{1,2},{2,3},{3,0},{4,5},{5,6},{6,7},{7,4},{8,9},{9,10},{10,1... | collective-permute-start | bytes 296408 | tf_op jit(solution)/shard_map/ppermute | solution.py:46
  100.2 0.7 copy-start.2
where the time goes:
time: 101 us
  waiting for transfers between devices  58.5 us (58%)
  starting transfers between devices  20.2 us (20%)
  other arithmetic  15.6 us (15%)
  local copies, waits for them, and re-layouts  4.86 us (5%)
  between operations  1.7 us (2%)
    ppermute x9, waiting for transfers between devices, with_halo(): lax.ppermute(lax.slice_in_dim(block, 0, width, axis=dim), axis, backward)  39.6 us
    ppermute x9, waiting for transfers between devices, with_halo(): lax.ppermute(lax.slice_in_dim(block, block.shape[dim] - width, None, axis...  18.9 us
    ppermute x9, starting transfers between devices, with_halo(): lax.ppermute(lax.slice_in_dim(block, 0, width, axis=dim), axis, backward)  13.8 us
    ppermute x9, starting transfers between devices, with_halo(): lax.ppermute(lax.slice_in_dim(block, block.shape[dim] - width, None, axis...  6.4 us
    unnamed x51, other arithmetic  4.05 us
    scatter-add x2, other arithmetic, collide(): bounced = current[jnp.asarray(opposite_index)]  3.81 us
    unnamed x25, local copies, waits for them, and re-layouts  2.82 us
    concatenate x6, other arithmetic, with_halo(): block = jnp.concatenate([low, block, high], axis=dim)  2.59 us
  transfers between devices with their start and end apart: 18, of which 12 were waited for; matrix products, arithmetic and copies ran while one was open for 4% of the time, Pallas kernels for 0%

commit v1 on v0

v1 whole, which is shorter than its diff:
```python
import functools
import math

import jax
import jax.numpy as jnp
from jax import lax
from jax.experimental import pallas as pl
from jax.experimental.pallas import tpu as pltpu
from jax.sharding import PartitionSpec as P

MESH = pl.DeviceIdType.MESH

VEL = (
    (0, 0, 0),
    (1, 0, 0),
    (-1, 0, 0),
    (0, 1, 0),
    (0, -1, 0),
    (0, 0, 1),
    (0, 0, -1),
    (1, 1, 0),
    (-1, -1, 0),
    (1, -1, 0),
    (-1, 1, 0),
    (1, 0, 1),
    (-1, 0, -1),
    (1, 0, -1),
    (-1, 0, 1),
    (0, 1, 1),
    (0, -1, -1),
    (0, 1, -1),
    (0, -1, 1),
)
Q = len(VEL)
WEIGHT = (1.0 / 3.0,) + (1.0 / 18.0,) * 6 + (1.0 / 36.0,) * 12
OPP = (0, 2, 1, 4, 3, 6, 5, 8, 7, 10, 9, 12, 11, 14, 13, 16, 15, 18, 17)
SIGNS = (1, -1)


def side(move):
    return 0 if move == 1 else 1


def moves(sign):
    return [tuple(sign * c for c in v) for v in VEL]


def order_along(which, sign):
    place = {}
    for way in SIGNS:
        count = 0
        for q, m in enumerate(moves(sign)):
            if m[which] == way:
                place[q] = count
                count += 1
    return place


def message_list(merge):
    out = []
    ys = (1,) if merge else SIGNS
    for ox in SIGNS:
        for oz in SIGNS:
            out.append(((ox, 0, oz), "x", (side(ox), 3 + side(oz))))
    for oz in SIGNS:
        for oy in ys:
            out.append(((0, oy, oz), "e", (side(oy), side(oz))))
    for ox in SIGNS:
        for oy in ys:
            out.append(((ox, oy, 0), "x", (side(ox), 1 + side(oy))))
    for oz in SIGNS:
        out.append(((0, 0, oz), "z", (side(oz),)))
    if merge:
        out.append(((0, 1, 0), "yy", ()))
    else:
        for oy in SIGNS:
            out.append(((0, oy, 0), "y", (side(oy),)))
    for ox in SIGNS:
        out.append(((ox, 0, 0), "x", (side(ox), 0)))
    return out


def total(items):
    items = list(items)
    while len(items) > 1:
        nxt = [items[i] + items[i + 1] for i in range(0, len(items) - 1, 2)]
        if len(items) % 2:
            nxt.append(items[-1])
        items = nxt
    return items[0]


def first_moments(f):
    density = total(f)
    flow = []
    for d in range(3):
        plus = total([f[q] for q in range(Q) if VEL[q][d] == 1])
        minus = total([f[q] for q in range(Q) if VEL[q][d] == -1])
        flow.append(plus - minus)
    return density, flow


def along(b):
    bx, by, bz = b
    return {
        1: bx, 3: by, 5: bz,
        7: bx + by, 9: bx - by, 11: bx + bz, 13: bx - bz, 15: by + bz, 17: by - bz,
    }


def collided(f, r, v, alpha, wall):
    vv = v[0] * v[0] + v[1] * v[1] + v[2] * v[2]
    base = 1.0 - 1.5 * vv
    out = [None] * Q
    out[0] = jnp.where(wall, f[0], alpha * f[0] + (WEIGHT[0] * r) * base)
    by_weight = {1: WEIGHT[1] * r, 2: WEIGHT[7] * r}
    for q, cv in along(v).items():
        wr = by_weight[1 if q < 7 else 2]
        even = wr * (base + 4.5 * (cv * cv))
        odd = wr * (3.0 * cv)
        out[q] = jnp.where(wall, f[q + 1], alpha * f[q] + (even + odd))
        out[q + 1] = jnp.where(wall, f[q], alpha * f[q + 1] + (even - odd))
    return out


def pulled_back(g, r, u, cells):
    alpha, beta, keep, damp, wall = cells
    v = [keep * x for x in u]
    sums = {q: g[q] + g[q + 1] for q in range(1, Q, 2)}
    diff = {q: g[q] - g[q + 1] for q in range(1, Q, 2)}
    wa, wb = WEIGHT[1], WEIGHT[7]
    axes = total([sums[1], sums[3], sums[5]])
    diag = total([sums[q] for q in (7, 9, 11, 13, 15, 17)])
    g0 = WEIGHT[0] * g[0] + wa * axes + wb * diag
    gx = wa * diff[1] + wb * ((diff[7] + diff[9]) + (diff[11] + diff[13]))
    gy = wa * diff[3] + wb * ((diff[7] - diff[9]) + (diff[15] + diff[17]))
    gz = wa * diff[5] + wb * ((diff[11] - diff[13]) + (diff[15] - diff[17]))
    xy, xz, yz = sums[7] + sums[9], sums[11] + sums[13], sums[15] + sums[17]
    gxx = wa * sums[1] + wb * (xy + xz)
    gyy = wa * sums[3] + wb * (xy + yz)
    gzz = wa * sums[5] + wb * (xz + yz)
    gxy = wb * (sums[7] - sums[9])
    gxz = wb * (sums[11] - sums[13])
    gyz = wb * (sums[15] - sums[17])
    hx = 4.5 * (gxx * v[0] + gxy * v[1] + gxz * v[2]) - 1.5 * g0 * v[0]
    hy = 4.5 * (gxy * v[0] + gyy * v[1] + gyz * v[2]) - 1.5 * g0 * v[1]
    hz = 4.5 * (gxz * v[0] + gyz * v[1] + gzz * v[2]) - 1.5 * g0 * v[2]
    slope = [3.0 * gx + 2.0 * hx, 3.0 * gy + 2.0 * hy, 3.0 * gz + 2.0 * hz]
    quad = v[0] * hx + v[1] * hy + v[2] * hz
    uu = u[0] * u[0] + u[1] * u[1] + u[2] * u[2]
    a0 = beta * (g0 - quad) - damp * uu
    scale = beta * keep
    twice = 2.0 * damp
    b = [scale * s + twice * x for s, x in zip(slope, u)]
    out = [None] * Q
    out[0] = jnp.where(wall, g[0], alpha * g[0] + a0)
    for q, cb in along(b).items():
        out[q] = jnp.where(wall, g[q + 1], alpha * g[q] + (a0 + cb))
        out[q + 1] = jnp.where(wall, g[q], alpha * g[q + 1] + (a0 - cb))
    by_damp = r * (uu - 1.25 * (slope[0] * u[0] + slope[1] * u[1] + slope[2] * u[2]))
    return out, by_damp


class Exchange:
    def __init__(self, signs, nz, refs):
        self.signs = signs
        self.nz = nz
        self.kept, self.px, self.py, self.pe, self.pz = refs[:5]
        self.rx, self.ry, self.re, self.rz = refs[5:]
        self.count = 5 * nz
        self.lane = lax.broadcasted_iota(jnp.int32, (8, 128), 1)
        self.row = lax.broadcasted_iota(jnp.int32, (8, 128), 0)
        zero = jnp.zeros((8, 128), jnp.float32)
        self.packed = [zero, zero]
        self.moves = [moves(s) for s in signs]
        self.places = [[order_along(d, s) for d in range(3)] for s in signs]

    def edge_row(self, fi, oy, oz):
        return (fi * 2 + side(oy)) * 2 + side(oz)

    def scatter(self, fi, z, tiles):
        nz = self.nz
        for q in range(Q):
            mx, my, mz = self.moves[fi][q]
            place = self.places[fi]
            t = tiles[q]
            if my:
                t = pltpu.roll(t, my % 8, axis=0)
            flat = t
            if mx:
                t = pltpu.roll(t, mx % 128, axis=1)
            zp = (z + mz) % nz
            wraps = zp != z + mz
            if wraps:
                self.pz[side(mz), fi * 5 + place[2][q]] = t
            else:
                self.kept[fi, q, zp] = t
            if mx:
                k = fi * self.count + place[0][q] * nz + zp
                moved = pltpu.roll(flat, (k + 1 if mx == 1 else k + 1 + 127) % 128, axis=1) \
                    if mx == 1 else pltpu.roll(flat, k % 128, axis=1) if k else flat
                s = side(mx)
                self.packed[s] = jnp.where(self.lane == k, moved, self.packed[s])
            if my:
                w = 0 if my == 1 else 7
                s = side(my)
                edge = t[w : w + 1, :]
                if wraps:
                    e = self.edge_row(fi, my, mz)
                    self.pe[e : e + 1, :] = edge
                else:
                    k = fi * self.count + place[1][q] * nz + zp
                    self.py[s, k : k + 1, :] = edge

    def pack(self):
        for s in (0, 1):
            self.px[s] = self.packed[s]

    def gather(self, fi, z, merge):
        nz = self.nz
        out = []
        for q in range(Q):
            mx, my, mz = self.moves[fi][q]
            place = self.places[fi]
            wraps = (mz == 1 and z == 0) or (mz == -1 and z == nz - 1)
            if wraps:
                t = self.rz[side(mz), fi * 5 + place[2][q]]
            else:
                t = self.kept[fi, q, z]
            sy = 0 if merge else side(my)
            w = 0 if my == 1 else 7
            if my:
                if wraps:
                    e = self.edge_row(fi, my, mz)
                    edge = self.re[sy, side(mz), e : e + 1, :]
                else:
                    k = fi * self.count + place[1][q] * nz + z
                    edge = self.ry[side(my), k : k + 1, :]
                t = jnp.where(self.row == w, jnp.broadcast_to(edge, (8, 128)), t)
            if mx:
                s = side(mx)
                k = fi * self.count + place[0][q] * nz + z
                if wraps:
                    col = self.rx[s, 3 + side(mz)]
                else:
                    col = self.rx[s, 0]
                    if my:
                        col = jnp.where(self.row == w, self.rx[s, 1 + sy], col)
                target = 0 if mx == 1 else 127
                shift = (target - k) % 128
                if shift:
                    col = pltpu.roll(col, shift, axis=1)
                t = jnp.where(self.lane == target, col, t)
            out.append(t)
        return out


def kernel(
    sizes, nz,
    step_ref, pop_hbm, por_hbm, kind_hbm, adj_hbm,
    out_ref, sens_ref,
    pop, por, kind, adj, saved, load_sem,
    kept1, px1, py1, pe1, pz1, rx1, ry1, re1, rz1,
    kept2, px2, py2, pe2, pz2, rx2, ry2, re2, rz2,
    send1, recv1, send2, recv2,
):
    merge = sizes[1] == 2
    names = ("gx", "gy", "gz")
    here = [lax.axis_index(n) for n in names]
    messages = message_list(merge)

    def target(offset):
        return {
            n: lax.rem(here[d] + (offset[d] + sizes[d]), sizes[d])
            for d, n in enumerate(names) if offset[d]
        }

    loads = [
        pltpu.make_async_copy(src, dst, load_sem.at[i])
        for i, (src, dst) in enumerate(
            ((adj_hbm, adj), (pop_hbm, pop), (por_hbm, por), (kind_hbm, kind))
        )
    ]
    for c in loads:
        c.start()
    barrier = pltpu.get_barrier_semaphore()
    for offset, _, _ in messages:
        pl.semaphore_signal(barrier, inc=1, device_id=target(offset), device_id_type=MESH)

    def copies(bufs, send, recv):
        px, py, pe, pz, rx, ry, re, rz = bufs
        made = []
        for i, (offset, what, at) in enumerate(messages):
            if what == "x":
                src, dst = px.at[at[0]], rx.at[at[0], at[1]]
            elif what == "e":
                src, dst = pe, re.at[at[0], at[1]]
            elif what == "z":
                src, dst = pz.at[at[0]], rz.at[at[0]]
            elif what == "yy":
                src, dst = py, ry
            else:
                src, dst = py.at[at[0]], ry.at[at[0]]
            made.append(pltpu.make_async_remote_copy(
                src_ref=src, dst_ref=dst, send_sem=send.at[i], recv_sem=recv.at[i],
                device_id=target(offset), device_id_type=MESH,
            ))
        return made

    first = Exchange((1, -1), nz, (kept1, px1, py1, pe1, pz1, rx1, ry1, re1, rz1))
    second = Exchange((-1,), nz, (kept2, px2, py2, pe2, pz2, rx2, ry2, re2, rz2))

    pe1[...] = jnp.zeros_like(pe1)
    py1[...] = jnp.zeros_like(py1)
    pe2[...] = jnp.zeros_like(pe2)
    py2[...] = jnp.zeros_like(py2)

    loads[0].wait()
    for z in range(nz):
        first.scatter(1, z, [adj[q, z] for q in range(Q)])

    moment = jnp.full((8, 128), jnp.bitwise_and(step_ref[0], 63), jnp.int32)
    angle = moment.astype(jnp.float32) * (2.0 * math.pi / 64.0)
    inlet_speed = 0.1 * (1.0 + 0.8 * jnp.sin(angle))
    zero = jnp.zeros((8, 128), jnp.float32)

    def cell_kinds(z):
        n = kind[z]
        fluid = n == 0
        outlet = n == 3
        denom = 0.1 + por[z]
        k = 0.1 * (1.0 - por[z]) / denom
        alpha = jnp.where(fluid, -0.25, 0.0)
        beta = jnp.where(fluid, 1.25, jnp.where(outlet, 1.0, 0.0))
        keep = jnp.where(fluid, 1.0 - k, 1.0)
        damp = jnp.where(fluid, k, 0.0)
        return n, (alpha, beta, keep, damp, n == 1), denom

    for c in loads[1:]:
        c.wait()
    for z in range(nz):
        n, cells, denom = cell_kinds(z)
        alpha, beta, keep, damp, wall = cells
        f = [pop[q, z] for q in range(Q)]
        r, flow = first_moments(f)
        u = [m / r for m in flow]
        inlet = n == 2
        v = [
            jnp.where(inlet, inlet_speed, keep * u[0]),
            jnp.where(inlet, zero, keep * u[1]),
            jnp.where(inlet, zero, keep * u[2]),
        ]
        first.scatter(0, z, collided(f, jnp.where(inlet, 1.0, beta * r), v, alpha, wall))
        saved[z, 0] = r
        for d in range(3):
            saved[z, 1 + d] = u[d]
        saved[z, 4] = keep
        saved[z, 5] = damp
        saved[z, 6] = jnp.where(n == 0, -0.11 / (denom * denom), 0.0)
    first.pack()
    pl.semaphore_wait(barrier, len(messages))
    sent1 = copies((px1, py1, pe1, pz1, rx1, ry1, re1, rz1), send1, recv1)
    for c in sent1:
        c.start()
    for c in sent1:
        c.wait_recv()

    def saved_cells(z):
        n = kind[z]
        fluid = n == 0
        alpha = jnp.where(fluid, -0.25, 0.0)
        beta = jnp.where(fluid, 1.25, jnp.where(n == 3, 1.0, 0.0))
        return alpha, beta, saved[z, 4], saved[z, 5], n == 1

    for z in range(nz):
        r, flow = first_moments(first.gather(0, z, merge))
        u = [m / r for m in flow]
        a, by_damp = pulled_back(first.gather(1, z, merge), r, u, saved_cells(z))
        sens_ref[z] = by_damp
        second.scatter(0, z, a)
    second.pack()
    sent2 = copies((px2, py2, pe2, pz2, rx2, ry2, re2, rz2), send2, recv2)
    for c in sent2:
        c.start()
    for c in sent2:
        c.wait_recv()
    for z in range(nz):
        u = [saved[z, 1 + d] for d in range(3)]
        a, by_damp = pulled_back(second.gather(0, z, merge), saved[z, 0], u, saved_cells(z))
        sens_ref[z] = saved[z, 6] * (sens_ref[z] + by_damp)
        for q in range(Q):
            out_ref[q, z] = a[q]
    for c in sent1:
        c.wait_send()
    for c in sent2:
        c.wait_send()


def buffers(fields, nz):
    rows = -(-fields * 5 * nz // 8) * 8
    f32 = jnp.float32
    return [
        pltpu.VMEM((fields, Q, nz, 8, 128), f32),
        pltpu.VMEM((2, 8, 128), f32),
        pltpu.VMEM((2, rows, 128), f32),
        pltpu.VMEM((8, 128), f32),
        pltpu.VMEM((2, fields * 5, 8, 128), f32),
        pltpu.VMEM((2, 5, 8, 128), f32),
        pltpu.VMEM((2, rows, 128), f32),
        pltpu.VMEM((2, 2, 8, 128), f32),
        pltpu.VMEM((2, fields * 5, 8, 128), f32),
    ]


def on_device(sizes, populations, porosity, node_type, step_index, adjoint_end):
    _, nz, ny, nx = populations.shape
    assert (ny, nx) == (8, 128) and 10 * nz <= 128
    f32 = jnp.float32
    count = len(message_list(sizes[1] == 2))
    any_space = pl.BlockSpec(memory_space=pl.ANY)
    vmem = pl.BlockSpec(memory_space=pltpu.VMEM)
    return pl.pallas_call(
        functools.partial(kernel, sizes, nz),
        out_shape=(
            jax.ShapeDtypeStruct(populations.shape, f32),
            jax.ShapeDtypeStruct(porosity.shape, f32),
        ),
        in_specs=[pl.BlockSpec(memory_space=pltpu.SMEM)] + [any_space] * 4,
        out_specs=(vmem, vmem),
        scratch_shapes=[
            pltpu.VMEM(populations.shape, f32),
            pltpu.VMEM(porosity.shape, f32),
            pltpu.VMEM(node_type.shape, jnp.int32),
            pltpu.VMEM(populations.shape, f32),
            pltpu.VMEM((nz, 7, 8, 128), f32),
            pltpu.SemaphoreType.DMA((4,)),
        ] + buffers(2, nz) + buffers(1, nz) + [pltpu.SemaphoreType.DMA((count,))] * 4,
        compiler_params=pltpu.CompilerParams(collective_id=0, has_side_effects=True),
    )(step_index, populations, porosity, node_type, adjoint_end)


def solution(mesh):
    sizes = tuple(mesh.shape[n] for n in ("gx", "gy", "gz"))
    return jax.shard_map(
        functools.partial(on_device, sizes),
        mesh=mesh,
        in_specs=(
            P(None, "gz", "gy", "gx"),
            P("gz", "gy", "gx"),
            P("gz", "gy", "gx"),
            P(),
            P(None, "gz", "gy", "gx"),
        ),
        out_specs=(P(None, "gz", "gy", "gx"), P("gz", "gy", "gx")),
        check_vma=False,
    )
```

time: 101 us -> 21.5 us (0.21)
  waiting for transfers between devices: 58.5 us -> 0 us
  starting transfers between devices: 20.2 us -> 0 us
  Pallas kernels: 0 us -> 17.7 us
  other arithmetic: 15.6 us -> 0 us
  local copies, waits for them, and re-layouts: 4.86 us -> 2.32 us
    ppermute x18 -> x0, waiting for transfers between devices: 58.5 us -> none  [the longest x9 39.6 us: with_halo(): lax.ppermute(lax.slice_in_dim(block, 0, width, axis=dim), axis, backward)]
    ppermute x18 -> x0, starting transfers between devices: 20.2 us -> none  [the longest x9 13.8 us: with_halo(): lax.ppermute(lax.slice_in_dim(block, 0, width, axis=dim), axis, backward)]
    pallas_call x0 -> x1, Pallas kernels: none -> 17.7 us  [on_device(): pl.pallas_call(functools.partial(kernel, sizes, nz), out_shape=(jax.Shape...]
    unnamed x51 -> x0, other arithmetic: 4.05 us -> none
    scatter-add x2 -> x0, other arithmetic: 3.81 us -> none  [collide(): bounced = current[jnp.asarray(opposite_index)]]
    concatenate x6 -> x0, other arithmetic: 2.59 us -> none  [with_halo(): block = jnp.concatenate([low, block, high], axis=dim)]
    gather x1 -> x0, local copies, waits for them, and re-layouts: 1.57 us -> none  [collide(): bounced = current[jnp.asarray(opposite_index)]]
    reduce_sum x4 -> x0, other arithmetic: 1.51 us -> none  [the longest x2 1.25 us: equilibrium(): 1.0 + 3.0 * projected + 4.5 * projected * projected - 1.5 * square]
  transfers between devices with their start and end apart: 18 -> 0, of which waited for: 12 -> 0; matrix products, arithmetic and copies ran while one was open for 4% -> 0% of each run, Pallas kernels for 0% -> 0%
where the time goes in v1:
time: 21.5 us; the launch traced here: 21.4 us
  Pallas kernels  17.7 us (82%)
  local copies, waits for them, and re-layouts  2.32 us (11%)
  between operations  1.29 us (6%)
    pallas_call x1, Pallas kernels, on_device(): pl.pallas_call(functools.partial(kernel, sizes, nz), out_shape=(jax.Shape...  17.7 us
    unnamed x4, local copies, waits for them, and re-layouts  2.32 us

profile of v1, /device:TPU:0, one launch (start us, length us, event | category | flops | bytes accessed | tf_op | source)
XLA Modules:
  0.0 21.4 jit_solution(3349379791663862887)
XLA Ops:
  1.3 17.7 %shard_map.68 = (f32[19,4,8,128]{3,2,1,0:T(8,128)}, f32[4,8,128]{2,1,0:T(8,128)}) custom-call(s32[1]{0:T(128)S(6)} %copy.9.step_ref, f32[19,4,8,128]{3,2,1,0:T(8,128)} %pop_hbm.1, f32[4,8,128]{2,1,0:T(8,128)} %por_hbm.1, s32[4,8,128]{2,1,0:T(8,128)} %kind_hbm.1, f32[19,4,8,128]{3,2,1,0:T(8,128)} %adj_hbm.1), custom_call_target="tpu_custom_call" | custom-call | tf_op jit(solution)/shard_map/pallas_call | solution.py:422
  19.0 0.0 copy-start
  19.0 1.7 %copy.10 = f32[19,4,8,128]{3,2,1,0:T(8,128)} copy(f32[19,4,8,128]{3,2,1,0:T(8,128)} %get-tuple-element.4) | data formatting | bytes 622592
  20.8 0.0 copy-done
  20.8 0.6 %copy.11 = f32[4,8,128]{2,1,0:T(8,128)} copy(f32[4,8,128]{2,1,0:T(8,128)S(1)} %copy-done) | data formatting | bytes 32768
Async XLA Ops:
  19.0 1.7 %copy-start = (f32[4,8,128]{2,1,0:T(8,128)S(1)}, f32[4,8,128]{2,1,0:T(8,128)}, u32[]{:S(2)}) copy-start(f32[4,8,128]{2,1,0:T(8,128)} %get-tuple-element.5) | copy-start | bytes 49156

commit v2 on v1

--- a/solution.py
+++ b/solution.py
@@ -57,27 +57,20 @@
 
 
 def message_list(merge):
+    ys = (1,) if merge else SIGNS
     out = []
-    ys = (1,) if merge else SIGNS
+    for oz in SIGNS:
+        out += [((ox, 0, oz), "xz", (side(ox), 3 + side(oz))) for ox in SIGNS]
+        out += [((0, oy, oz), "e", (side(oy), side(oz))) for oy in ys]
+        out.append(((0, 0, oz), "z", (side(oz),)))
     for ox in SIGNS:
-        for oz in SIGNS:
-            out.append(((ox, 0, oz), "x", (side(ox), 3 + side(oz))))
-    for oz in SIGNS:
-        for oy in ys:
-            out.append(((0, oy, oz), "e", (side(oy), side(oz))))
-    for ox in SIGNS:
-        for oy in ys:
-            out.append(((ox, oy, 0), "x", (side(ox), 1 + side(oy))))
-    for oz in SIGNS:
-        out.append(((0, 0, oz), "z", (side(oz),)))
-    if merge:
-        out.append(((0, 1, 0), "yy", ()))
-    else:
-        for oy in SIGNS:
-            out.append(((0, oy, 0), "y", (side(oy),)))
-    for ox in SIGNS:
-        out.append(((ox, 0, 0), "x", (side(ox), 0)))
+        out += [((ox, oy, 0), "x", (side(ox), 1 + side(oy))) for oy in ys]
+    out += [((0, oy, 0), "yy" if merge else "y", (side(oy),)) for oy in ys]
+    out += [((ox, 0, 0), "x", (side(ox), 0)) for ox in SIGNS]
     return out
+
+
+EARLY = ("xz", "e", "z")
 
 
 def total(items):
@@ -165,8 +158,8 @@
     def __init__(self, signs, nz, refs):
         self.signs = signs
         self.nz = nz
-        self.kept, self.px, self.py, self.pe, self.pz = refs[:5]
-        self.rx, self.ry, self.re, self.rz = refs[5:]
+        self.px, self.pq, self.py, self.pe, self.pz = refs[:5]
+        self.kept, self.rx, self.ry, self.re, self.rz = refs[5:]
         self.count = 5 * nz
         self.lane = lax.broadcasted_iota(jnp.int32, (8, 128), 1)
         self.row = lax.broadcasted_iota(jnp.int32, (8, 128), 0)
@@ -197,8 +190,8 @@
                 self.kept[fi, q, zp] = t
             if mx:
                 k = fi * self.count + place[0][q] * nz + zp
-                moved = pltpu.roll(flat, (k + 1 if mx == 1 else k + 1 + 127) % 128, axis=1) \
-                    if mx == 1 else pltpu.roll(flat, k % 128, axis=1) if k else flat
+                shift = k + 1 if mx == 1 else k
+                moved = pltpu.roll(flat, shift, axis=1) if shift else flat
                 s = side(mx)
                 self.packed[s] = jnp.where(self.lane == k, moved, self.packed[s])
             if my:
@@ -212,11 +205,11 @@
                     k = fi * self.count + place[1][q] * nz + zp
                     self.py[s, k : k + 1, :] = edge
 
-    def pack(self):
+    def pack(self, target):
         for s in (0, 1):
-            self.px[s] = self.packed[s]
-
-    def gather(self, fi, z, merge):
+            target[s] = self.packed[s]
+
+    def gather(self, fi, z, merge, given=None):
         nz = self.nz
         out = []
         for q in range(Q):
@@ -251,29 +244,44 @@
                 if shift:
                     col = pltpu.roll(col, shift, axis=1)
                 t = jnp.where(self.lane == target, col, t)
+            if given is not None and (my or wraps):
+                span, depth, tiles = given
+                mask = None
+                if my:
+                    mask = jnp.logical_and(self.row == w, span)
+                if wraps:
+                    whole = depth[side(mz)]
+                    mask = whole if mask is None else jnp.logical_or(mask, whole)
+                t = jnp.where(mask, tiles(OPP[q]), t)
             out.append(t)
         return out
 
 
-def kernel(
+def saved_cells(saved, kind, z):
+    n = kind[z]
+    fluid = n == 0
+    alpha = jnp.where(fluid, -0.25, 0.0)
+    beta = jnp.where(fluid, 1.25, jnp.where(n == 3, 1.0, 0.0))
+    return alpha, beta, saved[z, 4], saved[z, 5], n == 1
+
+
+def depth_order(nz):
+    return [0, nz - 1] + list(range(1, nz - 1))
+
+
+def window(
     sizes, nz,
-    step_ref, pop_hbm, por_hbm, kind_hbm, adj_hbm,
-    out_ref, sens_ref,
-    pop, por, kind, adj, saved, load_sem,
-    kept1, px1, py1, pe1, pz1, rx1, ry1, re1, rz1,
-    kept2, px2, py2, pe2, pz2, rx2, ry2, re2, rz2,
+    step, pop_hbm, por_hbm, kind_hbm, adj_hbm,
+    adj, kind, saved, part, edges, kept2, rx2, ry2, re2, rz2,
+    pop, por, load_sem,
+    px1, pq1, py1, pe1, pz1, px2, pq2, py2, pe2, pz2,
+    kept1, rx1, ry1, re1, rz1,
     send1, recv1, send2, recv2,
 ):
     merge = sizes[1] == 2
     names = ("gx", "gy", "gz")
     here = [lax.axis_index(n) for n in names]
     messages = message_list(merge)
-
-    def target(offset):
-        return {
-            n: lax.rem(here[d] + (offset[d] + sizes[d]), sizes[d])
-            for d, n in enumerate(names) if offset[d]
-        }
 
     loads = [
         pltpu.make_async_copy(src, dst, load_sem.at[i])
@@ -283,68 +291,115 @@
     ]
     for c in loads:
         c.start()
+
+    def target(offset):
+        return {
+            n: lax.rem(here[d] + (offset[d] + sizes[d]), sizes[d])
+            for d, n in enumerate(names) if offset[d]
+        }
+
+    def inside(offset, way):
+        ok = None
+        for d in (1, 2):
+            if offset[d] and not (d == 1 and merge):
+                place = here[d] + way * offset[d]
+                test = place < sizes[d] if way * offset[d] > 0 else place >= 0
+                ok = test if ok is None else jnp.logical_and(ok, test)
+        return ok
+
+    def guarded(ok, act):
+        if ok is None:
+            act()
+        else:
+            pl.when(ok)(act)
+
     barrier = pltpu.get_barrier_semaphore()
+    expected = 0
     for offset, _, _ in messages:
-        pl.semaphore_signal(barrier, inc=1, device_id=target(offset), device_id_type=MESH)
+        guarded(inside(offset, 1), lambda offset=offset: pl.semaphore_signal(
+            barrier, inc=1, device_id=target(offset), device_id_type=MESH))
+        ok = inside(offset, -1)
+        expected = expected + (1 if ok is None else jnp.where(ok, 1, 0))
 
     def copies(bufs, send, recv):
-        px, py, pe, pz, rx, ry, re, rz = bufs
+        px, pq, py, pe, pz, rx, ry, re, rz = bufs
         made = []
         for i, (offset, what, at) in enumerate(messages):
             if what == "x":
                 src, dst = px.at[at[0]], rx.at[at[0], at[1]]
+            elif what == "xz":
+                src, dst = pq.at[at[0]], rx.at[at[0], at[1]]
             elif what == "e":
                 src, dst = pe, re.at[at[0], at[1]]
             elif what == "z":
                 src, dst = pz.at[at[0]], rz.at[at[0]]
             elif what == "yy":
-                src, dst = py, ry
+                src, dst = py.at[here[1]], ry.at[here[1]]
             else:
                 src, dst = py.at[at[0]], ry.at[at[0]]
-            made.append(pltpu.make_async_remote_copy(
+            made.append((what in EARLY, offset, pltpu.make_async_remote_copy(
                 src_ref=src, dst_ref=dst, send_sem=send.at[i], recv_sem=recv.at[i],
                 device_id=target(offset), device_id_type=MESH,
-            ))
+            )))
         return made
 
-    first = Exchange((1, -1), nz, (kept1, px1, py1, pe1, pz1, rx1, ry1, re1, rz1))
-    second = Exchange((-1,), nz, (kept2, px2, py2, pe2, pz2, rx2, ry2, re2, rz2))
+    def start(made, early):
+        for when, offset, c in made:
+            if when == early:
+                guarded(inside(offset, 1), c.start)
+
+    def arrive(made):
+        for _, offset, c in made:
+            guarded(inside(offset, -1), c.wait_recv)
+
+    def leave(made):
+        for _, offset, c in made:
+            guarded(inside(offset, 1), c.wait_send)
+
+    first = Exchange((1, -1), nz, (px1, pq1, py1, pe1, pz1, kept1, rx1, ry1, re1, rz1))
+    second = Exchange((-1,), nz, (px2, pq2, py2, pe2, pz2, kept2, rx2, ry2, re2, rz2))
 
     pe1[...] = jnp.zeros_like(pe1)
     py1[...] = jnp.zeros_like(py1)
     pe2[...] = jnp.zeros_like(pe2)
     py2[...] = jnp.zeros_like(py2)
 
+    row = first.row
+    span = jnp.logical_or(
+        jnp.logical_and(row == 0, jnp.full((8, 128), here[1], jnp.int32) == 0),
+        jnp.logical_and(row == 7, jnp.full((8, 128), here[1], jnp.int32) == sizes[1] - 1),
+    )
+    depth = jnp.full((8, 128), here[2], jnp.int32)
+    edges[0] = jnp.where(span, 1, 0)
+    edges[1] = jnp.where(depth == 0, 1, 0)
+    edges[2] = jnp.where(depth == sizes[2] - 1, 1, 0)
+
     loads[0].wait()
-    for z in range(nz):
+    for z in depth_order(nz):
         first.scatter(1, z, [adj[q, z] for q in range(Q)])
 
-    moment = jnp.full((8, 128), jnp.bitwise_and(step_ref[0], 63), jnp.int32)
+    for c in loads[1:]:
+        c.wait()
+    moment = jnp.full((8, 128), jnp.bitwise_and(step[0], 63), jnp.int32)
     angle = moment.astype(jnp.float32) * (2.0 * math.pi / 64.0)
     inlet_speed = 0.1 * (1.0 + 0.8 * jnp.sin(angle))
     zero = jnp.zeros((8, 128), jnp.float32)
 
-    def cell_kinds(z):
+    sent1 = copies((px1, pq1, py1, pe1, pz1, rx1, ry1, re1, rz1), send1, recv1)
+    sent2 = copies((px2, pq2, py2, pe2, pz2, rx2, ry2, re2, rz2), send2, recv2)
+    for turn, z in enumerate(depth_order(nz)):
         n = kind[z]
         fluid = n == 0
-        outlet = n == 3
+        inlet = n == 2
+        wall = n == 1
         denom = 0.1 + por[z]
         k = 0.1 * (1.0 - por[z]) / denom
         alpha = jnp.where(fluid, -0.25, 0.0)
-        beta = jnp.where(fluid, 1.25, jnp.where(outlet, 1.0, 0.0))
+        beta = jnp.where(fluid, 1.25, jnp.where(n == 3, 1.0, 0.0))
         keep = jnp.where(fluid, 1.0 - k, 1.0)
-        damp = jnp.where(fluid, k, 0.0)
-        return n, (alpha, beta, keep, damp, n == 1), denom
-
-    for c in loads[1:]:
-        c.wait()
-    for z in range(nz):
-        n, cells, denom = cell_kinds(z)
-        alpha, beta, keep, damp, wall = cells
         f = [pop[q, z] for q in range(Q)]
         r, flow = first_moments(f)
         u = [m / r for m in flow]
-        inlet = n == 2
         v = [
             jnp.where(inlet, inlet_speed, keep * u[0]),
             jnp.where(inlet, zero, keep * u[1]),
@@ -355,88 +410,127 @@
         for d in range(3):
             saved[z, 1 + d] = u[d]
         saved[z, 4] = keep
-        saved[z, 5] = damp
-        saved[z, 6] = jnp.where(n == 0, -0.11 / (denom * denom), 0.0)
-    first.pack()
-    pl.semaphore_wait(barrier, len(messages))
-    sent1 = copies((px1, py1, pe1, pz1, rx1, ry1, re1, rz1), send1, recv1)
-    for c in sent1:
-        c.start()
-    for c in sent1:
-        c.wait_recv()
-
-    def saved_cells(z):
-        n = kind[z]
-        fluid = n == 0
-        alpha = jnp.where(fluid, -0.25, 0.0)
-        beta = jnp.where(fluid, 1.25, jnp.where(n == 3, 1.0, 0.0))
-        return alpha, beta, saved[z, 4], saved[z, 5], n == 1
-
-    for z in range(nz):
+        saved[z, 5] = jnp.where(fluid, k, 0.0)
+        saved[z, 6] = -0.11 / (denom * denom)
+        if turn == 1:
+            first.pack(pq1)
+            pl.semaphore_wait(barrier, expected)
+            start(sent1, True)
+    first.pack(px1)
+    start(sent1, False)
+    arrive(sent1)
+
+    for turn, z in enumerate(depth_order(nz)):
         r, flow = first_moments(first.gather(0, z, merge))
         u = [m / r for m in flow]
-        a, by_damp = pulled_back(first.gather(1, z, merge), r, u, saved_cells(z))
-        sens_ref[z] = by_damp
+        a, by_damp = pulled_back(
+            first.gather(1, z, merge), r, u, saved_cells(saved, kind, z))
+        part[z] = by_damp
         second.scatter(0, z, a)
-    second.pack()
-    sent2 = copies((px2, py2, pe2, pz2, rx2, ry2, re2, rz2), send2, recv2)
-    for c in sent2:
+        if turn == 1:
+            second.pack(pq2)
+            start(sent2, True)
+    second.pack(px2)
+    start(sent2, False)
+    leave(sent1)
+    arrive(sent2)
+    leave(sent2)
+
+
+def last_step(
+    merge, nz,
+    adj, kind, saved, part, edges, kept, rx, ry, re, rz,
+    out_hbm, sens_hbm,
+    out, sens, out_sem, sens_sem,
+):
+    field = Exchange((-1,), nz, (None,) * 5 + (kept, rx, ry, re, rz))
+    span = edges[0] == 1
+    depth = (edges[1] == 1, edges[2] == 1)
+    copies = []
+    for z in range(nz):
+        g = field.gather(0, z, merge, (span, depth, lambda q, z=z: adj[q, z]))
+        u = [saved[z, 1 + d] for d in range(3)]
+        a, by_damp = pulled_back(g, saved[z, 0], u, saved_cells(saved, kind, z))
+        sens[z] = jnp.where(kind[z] == 0, saved[z, 6] * (part[z] + by_damp), 0.0)
+        for q in range(Q):
+            out[q, z] = a[q]
+        c = pltpu.make_async_copy(out.at[:, z], out_hbm.at[:, z], out_sem.at[z])
         c.start()
-    for c in sent2:
-        c.wait_recv()
-    for z in range(nz):
-        u = [saved[z, 1 + d] for d in range(3)]
-        a, by_damp = pulled_back(second.gather(0, z, merge), saved[z, 0], u, saved_cells(z))
-        sens_ref[z] = saved[z, 6] * (sens_ref[z] + by_damp)
-        for q in range(Q):
-            out_ref[q, z] = a[q]
-    for c in sent1:
-        c.wait_send()
-    for c in sent2:
-        c.wait_send()
-
-
-def buffers(fields, nz):
+        copies.append(c)
+    c = pltpu.make_async_copy(sens, sens_hbm, sens_sem)
+    c.start()
+    copies.append(c)
+    for c in copies:
+        c.wait()
+
+
+def packed_shapes(fields, nz):
     rows = -(-fields * 5 * nz // 8) * 8
-    f32 = jnp.float32
     return [
-        pltpu.VMEM((fields, Q, nz, 8, 128), f32),
-        pltpu.VMEM((2, 8, 128), f32),
-        pltpu.VMEM((2, rows, 128), f32),
-        pltpu.VMEM((8, 128), f32),
-        pltpu.VMEM((2, fields * 5, 8, 128), f32),
-        pltpu.VMEM((2, 5, 8, 128), f32),
-        pltpu.VMEM((2, rows, 128), f32),
-        pltpu.VMEM((2, 2, 8, 128), f32),
-        pltpu.VMEM((2, fields * 5, 8, 128), f32),
+        (2, 8, 128), (2, 8, 128), (2, rows, 128), (8, 128), (2, fields * 5, 8, 128),
     ]
+
+
+def landing_shapes(fields, nz):
+    rows = -(-fields * 5 * nz // 8) * 8
+    return [
+        (fields, Q, nz, 8, 128), (2, 5, 8, 128), (2, rows, 128), (2, 2, 8, 128),
+        (2, fields * 5, 8, 128),
+    ]
+
+
+LIMIT = 8 * 1024 * 1024
 
 
 def on_device(sizes, populations, porosity, node_type, step_index, adjoint_end):
     _, nz, ny, nx = populations.shape
-    assert (ny, nx) == (8, 128) and 10 * nz <= 128
+    assert (ny, nx) == (8, 128) and nz >= 2 and 10 * nz <= 128
     f32 = jnp.float32
-    count = len(message_list(sizes[1] == 2))
+    i32 = jnp.int32
+    merge = sizes[1] == 2
+    count = len(message_list(merge))
     any_space = pl.BlockSpec(memory_space=pl.ANY)
     vmem = pl.BlockSpec(memory_space=pltpu.VMEM)
+    handed = [
+        pltpu.VMEM(populations.shape, f32),
+        pltpu.VMEM(node_type.shape, i32),
+        pltpu.VMEM((nz, 7, 8, 128), f32),
+        pltpu.VMEM(porosity.shape, f32),
+        pltpu.VMEM((3, 8, 128), i32),
+    ] + [pltpu.VMEM(s, f32) for s in landing_shapes(1, nz)]
+    scratch = packed_shapes(2, nz) + packed_shapes(1, nz) + landing_shapes(2, nz)
+    state = pl.pallas_call(
+        functools.partial(window, sizes, nz),
+        out_shape=handed,
+        in_specs=[pl.BlockSpec(memory_space=pltpu.SMEM)] + [pl.BlockSpec(memory_space=pltpu.HBM)] * 4,
+        out_specs=[vmem] * len(handed),
+        scratch_shapes=[
+            pltpu.VMEM(populations.shape, f32),
+            pltpu.VMEM(porosity.shape, f32),
+            pltpu.SemaphoreType.DMA((4,)),
+        ] + [pltpu.VMEM(s, f32) for s in scratch] + [pltpu.SemaphoreType.DMA((count,))] * 4,
+        compiler_params=pltpu.CompilerParams(
+            collective_id=0, has_side_effects=True, vmem_limit_bytes=LIMIT),
+    )(step_index, *[
+        pltpu.with_memory_space_constraint(x, pltpu.HBM)
+        for x in (populations, porosity, node_type, adjoint_end)
+    ])
     return pl.pallas_call(
-        functools.partial(kernel, sizes, nz),
+        functools.partial(last_step, merge, nz),
         out_shape=(
             jax.ShapeDtypeStruct(populations.shape, f32),
             jax.ShapeDtypeStruct(porosity.shape, f32),
         ),
-        in_specs=[pl.BlockSpec(memory_space=pltpu.SMEM)] + [any_space] * 4,
-        out_specs=(vmem, vmem),
+        in_specs=[vmem] * len(handed),
+        out_specs=(any_space, any_space),
         scratch_shapes=[
             pltpu.VMEM(populations.shape, f32),
             pltpu.VMEM(porosity.shape, f32),
-            pltpu.VMEM(node_type.shape, jnp.int32),
-            pltpu.VMEM(populations.shape, f32),
-            pltpu.VMEM((nz, 7, 8, 128), f32),
-            pltpu.SemaphoreType.DMA((4,)),
-        ] + buffers(2, nz) + buffers(1, nz) + [pltpu.SemaphoreType.DMA((count,))] * 4,
-        compiler_params=pltpu.CompilerParams(collective_id=0, has_side_effects=True),
-    )(step_index, populations, porosity, node_type, adjoint_end)
+            pltpu.SemaphoreType.DMA((nz,)),
+            pltpu.SemaphoreType.DMA,
+        ],
+        compiler_params=pltpu.CompilerParams(vmem_limit_bytes=LIMIT),
+    )(*state)
 
 
 def solution(mesh):

time: 21.5 us -> 15 us (0.70)
  Pallas kernels: 17.7 us -> 13.6 us
  local copies, waits for them, and re-layouts: 2.32 us -> 0 us
    pallas_call x1 -> x2, Pallas kernels: 17.7 us -> 13.6 us  [the longest x1 12.7 us: on_device(): pl.pallas_call(functools.partial(window, sizes, nz), out_shape=handed, in...]
    unnamed x4 -> x0, local copies, waits for them, and re-layouts: 2.32 us -> none
where the time goes in v2:
time: 15 us; the launch traced here: 14.9 us
  Pallas kernels  13.6 us (91%)
  between operations  1.28 us (9%)
    pallas_call x1, Pallas kernels, on_device(): pl.pallas_call(functools.partial(window, sizes, nz), out_shape=handed, in...  12.7 us
    pallas_call x1, Pallas kernels, on_device(): pl.pallas_call(functools.partial(last_step, merge, nz), out_shape=(jax.Sh...  0.9 us

profile of v2, /device:TPU:0, one launch (start us, length us, event | category | flops | bytes accessed | tf_op | source)
XLA Modules:
  0.0 14.9 jit_solution(10081235770099774247)
XLA Ops:
  1.3 12.7 %shard_map.68 = (f32[19,4,8,128]{3,2,1,0:T(8,128)S(1)}, s32[4,8,128]{2,1,0:T(8,128)S(1)}, f32[4,7,8,128]{3,2,1,0:T(8,128)S(1)}, f32[4,8,128]{2,1,0:T(8,128)S(1)}...) custom-call(s32[1]{0:T(128)S(6)} %copy.7.step, ...), custom_call_target="tpu_custom_call" | custom-call | tf_op jit(solution)/shard_map/pallas_call | solution.py:502
  14.0 0.9 %shard_map.69 = (f32[19,4,8,128]{3,2,1,0:T(8,128)}, f32[4,8,128]{2,1,0:T(8,128)}) custom-call(f32[19,4,8,128]{3,2,1,0:T(8,128)S(1)} %get-tuple-element.12.adj, s32[4,8,128]{2,1,0:T(8,128)S(1)} %get-tuple-element.13.kind, f32[4,7,8,128]{3,2,1,0:T(8,128)S(1)} %get-tuple-element.14.saved, f32[4,8,128]{2,1,0:T(8,128)S(1)} %get-tuple-element.15.part, ...), custom_call_target="tpu_custom_call" | custom-call | tf_op jit(solution)/shard_map/pallas_call | solution.py:518

commit v3 on v2

--- a/solution.py
+++ b/solution.py
@@ -283,11 +283,12 @@
     here = [lax.axis_index(n) for n in names]
     messages = message_list(merge)
 
+    pairs = [(por_hbm, por), (kind_hbm, kind)]
+    for z in depth_order(nz):
+        pairs.append((adj_hbm.at[:, z], adj.at[:, z]))
+        pairs.append((pop_hbm.at[:, z], pop.at[:, z]))
     loads = [
-        pltpu.make_async_copy(src, dst, load_sem.at[i])
-        for i, (src, dst) in enumerate(
-            ((adj_hbm, adj), (pop_hbm, pop), (por_hbm, por), (kind_hbm, kind))
-        )
+        pltpu.make_async_copy(src, dst, load_sem.at[i]) for i, (src, dst) in enumerate(pairs)
     ]
     for c in loads:
         c.start()
@@ -298,27 +299,38 @@
             for d, n in enumerate(names) if offset[d]
         }
 
-    def inside(offset, way):
+    def bounded(offset):
+        return (0 if merge else offset[1], offset[2])
+
+    def inside(steps, way):
         ok = None
-        for d in (1, 2):
-            if offset[d] and not (d == 1 and merge):
-                place = here[d] + way * offset[d]
-                test = place < sizes[d] if way * offset[d] > 0 else place >= 0
+        for d, move in zip((1, 2), steps):
+            if move:
+                place = here[d] + way * move
+                test = place < sizes[d] if way * move > 0 else place >= 0
                 ok = test if ok is None else jnp.logical_and(ok, test)
         return ok
 
-    def guarded(ok, act):
-        if ok is None:
-            act()
-        else:
-            pl.when(ok)(act)
+    def guarded(items, way, act):
+        groups = {}
+        for item in items:
+            groups.setdefault(bounded(item[0]), []).append(item)
+        for steps, group in groups.items():
+            def every(group=group):
+                for item in group:
+                    act(item)
+            ok = inside(steps, way)
+            if ok is None:
+                every()
+            else:
+                pl.when(ok)(every)
 
     barrier = pltpu.get_barrier_semaphore()
+    guarded(messages, 1, lambda m: pl.semaphore_signal(
+        barrier, inc=1, device_id=target(m[0]), device_id_type=MESH))
     expected = 0
     for offset, _, _ in messages:
-        guarded(inside(offset, 1), lambda offset=offset: pl.semaphore_signal(
-            barrier, inc=1, device_id=target(offset), device_id_type=MESH))
-        ok = inside(offset, -1)
+        ok = inside(bounded(offset), -1)
         expected = expected + (1 if ok is None else jnp.where(ok, 1, 0))
 
     def copies(bufs, send, recv):
@@ -337,24 +349,20 @@
                 src, dst = py.at[here[1]], ry.at[here[1]]
             else:
                 src, dst = py.at[at[0]], ry.at[at[0]]
-            made.append((what in EARLY, offset, pltpu.make_async_remote_copy(
+            made.append((offset, what in EARLY, pltpu.make_async_remote_copy(
                 src_ref=src, dst_ref=dst, send_sem=send.at[i], recv_sem=recv.at[i],
                 device_id=target(offset), device_id_type=MESH,
             )))
         return made
 
     def start(made, early):
-        for when, offset, c in made:
-            if when == early:
-                guarded(inside(offset, 1), c.start)
+        guarded([m for m in made if m[1] == early], 1, lambda m: m[2].start())
 
     def arrive(made):
-        for _, offset, c in made:
-            guarded(inside(offset, -1), c.wait_recv)
+        guarded(made, -1, lambda m: m[2].wait_recv())
 
     def leave(made):
-        for _, offset, c in made:
-            guarded(inside(offset, 1), c.wait_send)
+        guarded(made, 1, lambda m: m[2].wait_send())
 
     first = Exchange((1, -1), nz, (px1, pq1, py1, pe1, pz1, kept1, rx1, ry1, re1, rz1))
     second = Exchange((-1,), nz, (px2, pq2, py2, pe2, pz2, kept2, rx2, ry2, re2, rz2))
@@ -374,12 +382,6 @@
     edges[1] = jnp.where(depth == 0, 1, 0)
     edges[2] = jnp.where(depth == sizes[2] - 1, 1, 0)
 
-    loads[0].wait()
-    for z in depth_order(nz):
-        first.scatter(1, z, [adj[q, z] for q in range(Q)])
-
-    for c in loads[1:]:
-        c.wait()
     moment = jnp.full((8, 128), jnp.bitwise_and(step[0], 63), jnp.int32)
     angle = moment.astype(jnp.float32) * (2.0 * math.pi / 64.0)
     inlet_speed = 0.1 * (1.0 + 0.8 * jnp.sin(angle))
@@ -387,7 +389,12 @@
 
     sent1 = copies((px1, pq1, py1, pe1, pz1, rx1, ry1, re1, rz1), send1, recv1)
     sent2 = copies((px2, pq2, py2, pe2, pz2, rx2, ry2, re2, rz2), send2, recv2)
+    loads[0].wait()
+    loads[1].wait()
     for turn, z in enumerate(depth_order(nz)):
+        loads[2 + 2 * turn].wait()
+        first.scatter(1, z, [adj[q, z] for q in range(Q)])
+        loads[3 + 2 * turn].wait()
         n = kind[z]
         fluid = n == 0
         inlet = n == 2
@@ -507,7 +514,7 @@
         scratch_shapes=[
             pltpu.VMEM(populations.shape, f32),
             pltpu.VMEM(porosity.shape, f32),
-            pltpu.SemaphoreType.DMA((4,)),
+            pltpu.SemaphoreType.DMA((2 + 2 * nz,)),
         ] + [pltpu.VMEM(s, f32) for s in scratch] + [pltpu.SemaphoreType.DMA((count,))] * 4,
         compiler_params=pltpu.CompilerParams(
             collective_id=0, has_side_effects=True, vmem_limit_bytes=LIMIT),

time: 15 us -> 15.2 us (1.013); the launches traced: 14.9 us -> 14.9 us
  no operation moved by 1% of the time
where the time goes in v3:
time: 15.2 us; the launch traced here: 14.9 us
  Pallas kernels  13.7 us (90%)
  between operations  1.28 us (8%)
    pallas_call x1, Pallas kernels, on_device(): pl.pallas_call(functools.partial(window, sizes, nz), out_shape=handed, in...  12.8 us
    pallas_call x1, Pallas kernels, on_device(): pl.pallas_call(functools.partial(last_step, merge, nz), out_shape=(jax.Sh...  0.9 us

profile of v3, /device:TPU:0, one launch (start us, length us, event | category | flops | bytes accessed | tf_op | source)
XLA Modules:
  0.0 14.9 jit_solution(10180412604046865074)
XLA Ops:
  1.3 12.8 %shard_map.68 = (f32[19,4,8,128]{3,2,1,0:T(8,128)S(1)}, s32[4,8,128]{2,1,0:T(8,128)S(1)}, f32[4,7,8,128]{3,2,1,0:T(8,128)S(1)}, f32[4,8,128]{2,1,0:T(8,128)S(1)}...) custom-call(s32[1]{0:T(128)S(6)} %copy.7.step, ...), custom_call_target="tpu_custom_call" | custom-call | tf_op jit(solution)/shard_map/pallas_call | solution.py:509
  14.0 0.9 %shard_map.69 = (f32[19,4,8,128]{3,2,1,0:T(8,128)}, f32[4,8,128]{2,1,0:T(8,128)}) custom-call(f32[19,4,8,128]{3,2,1,0:T(8,128)S(1)} %get-tuple-element.12.adj, s32[4,8,128]{2,1,0:T(8,128)S(1)} %get-tuple-element.13.kind, f32[4,7,8,128]{3,2,1,0:T(8,128)S(1)} %get-tuple-element.14.saved, f32[4,8,128]{2,1,0:T(8,128)S(1)} %get-tuple-element.15.part, ...), custom_call_target="tpu_custom_call" | custom-call | tf_op jit(solution)/shard_map/pallas_call | solution.py:525

commit v4 on v3

--- a/solution.py
+++ b/solution.py
@@ -56,21 +56,31 @@
     return place
 
 
-def message_list(merge):
+def message_list(merge, fields):
     ys = (1,) if merge else SIGNS
     out = []
+    for fi in reversed(range(fields)):
+        for oz in SIGNS:
+            stage = 0 if fi else 1 + (oz == 1)
+            out.append(((0, 0, oz), "z", (side(oz), fi), stage))
+        for oy in ys:
+            stage = 0 if fi else 3
+            out.append(((0, oy, 0), "yy" if merge else "y", (side(oy), fi), stage))
     for oz in SIGNS:
-        out += [((ox, 0, oz), "xz", (side(ox), 3 + side(oz))) for ox in SIGNS]
-        out += [((0, oy, oz), "e", (side(oy), side(oz))) for oy in ys]
-        out.append(((0, 0, oz), "z", (side(oz),)))
+        stage = 1 + (oz == 1)
+        out += [((ox, 0, oz), "xz", (side(ox), side(oz)), stage) for ox in SIGNS]
+        out += [((0, oy, oz), "e", (side(oy), side(oz)), stage) for oy in ys]
     for ox in SIGNS:
-        out += [((ox, oy, 0), "x", (side(ox), 1 + side(oy))) for oy in ys]
-    out += [((0, oy, 0), "yy" if merge else "y", (side(oy),)) for oy in ys]
-    out += [((ox, 0, 0), "x", (side(ox), 0)) for ox in SIGNS]
-    return out
-
-
-EARLY = ("xz", "e", "z")
+        out += [((ox, oy, 0), "x", (side(ox), 1 + side(oy)), 3) for oy in ys]
+    out += [((ox, 0, 0), "x", (side(ox), 0), 3) for ox in SIGNS]
+    rank = {"xz": 0, "e": 1, "z": 2, "x": 3, "yy": 4, "y": 4}
+    last = {(0, 0): 5}
+    return sorted(out, key=lambda m: (
+        m[3], last.get(m[0][1:], rank[m[1]]) if m[1] == "x" else rank[m[1]]))
+
+
+def face_rows(nz):
+    return -(-5 * nz // 8) * 8
 
 
 def total(items):
@@ -161,6 +171,7 @@
         self.px, self.pq, self.py, self.pe, self.pz = refs[:5]
         self.kept, self.rx, self.ry, self.re, self.rz = refs[5:]
         self.count = 5 * nz
+        self.rows = face_rows(nz)
         self.lane = lax.broadcasted_iota(jnp.int32, (8, 128), 1)
         self.row = lax.broadcasted_iota(jnp.int32, (8, 128), 0)
         zero = jnp.zeros((8, 128), jnp.float32)
@@ -168,8 +179,8 @@
         self.moves = [moves(s) for s in signs]
         self.places = [[order_along(d, s) for d in range(3)] for s in signs]
 
-    def edge_row(self, fi, oy, oz):
-        return (fi * 2 + side(oy)) * 2 + side(oz)
+    def edge_row(self, fi, oy):
+        return fi * 2 + side(oy)
 
     def scatter(self, fi, z, tiles):
         nz = self.nz
@@ -199,15 +210,15 @@
                 s = side(my)
                 edge = t[w : w + 1, :]
                 if wraps:
-                    e = self.edge_row(fi, my, mz)
-                    self.pe[e : e + 1, :] = edge
+                    e = self.edge_row(fi, my)
+                    self.pe[side(mz), e : e + 1, :] = edge
                 else:
-                    k = fi * self.count + place[1][q] * nz + zp
+                    k = fi * self.rows + place[1][q] * nz + zp
                     self.py[s, k : k + 1, :] = edge
 
-    def pack(self, target):
+    def pack(self, target, *at):
         for s in (0, 1):
-            target[s] = self.packed[s]
+            target[(*at, s)] = self.packed[s]
 
     def gather(self, fi, z, merge, given=None):
         nz = self.nz
@@ -224,10 +235,10 @@
             w = 0 if my == 1 else 7
             if my:
                 if wraps:
-                    e = self.edge_row(fi, my, mz)
+                    e = self.edge_row(fi, my)
                     edge = self.re[sy, side(mz), e : e + 1, :]
                 else:
-                    k = fi * self.count + place[1][q] * nz + z
+                    k = fi * self.rows + place[1][q] * nz + z
                     edge = self.ry[side(my), k : k + 1, :]
                 t = jnp.where(self.row == w, jnp.broadcast_to(edge, (8, 128)), t)
             if mx:
@@ -281,12 +292,11 @@
     merge = sizes[1] == 2
     names = ("gx", "gy", "gz")
     here = [lax.axis_index(n) for n in names]
-    messages = message_list(merge)
-
-    pairs = [(por_hbm, por), (kind_hbm, kind)]
-    for z in depth_order(nz):
-        pairs.append((adj_hbm.at[:, z], adj.at[:, z]))
-        pairs.append((pop_hbm.at[:, z], pop.at[:, z]))
+    both, alone = message_list(merge, 2), message_list(merge, 1)
+
+    pairs = [(adj_hbm.at[:, z], adj.at[:, z]) for z in depth_order(nz)]
+    pairs += [(por_hbm, por), (kind_hbm, kind)]
+    pairs += [(pop_hbm.at[:, z], pop.at[:, z]) for z in depth_order(nz)]
     loads = [
         pltpu.make_async_copy(src, dst, load_sem.at[i]) for i, (src, dst) in enumerate(pairs)
     ]
@@ -326,37 +336,38 @@
                 pl.when(ok)(every)
 
     barrier = pltpu.get_barrier_semaphore()
-    guarded(messages, 1, lambda m: pl.semaphore_signal(
+    guarded(alone, 1, lambda m: pl.semaphore_signal(
         barrier, inc=1, device_id=target(m[0]), device_id_type=MESH))
     expected = 0
-    for offset, _, _ in messages:
+    for offset, _, _, _ in alone:
         ok = inside(bounded(offset), -1)
         expected = expected + (1 if ok is None else jnp.where(ok, 1, 0))
 
-    def copies(bufs, send, recv):
+    def copies(messages, bufs, send, recv):
         px, pq, py, pe, pz, rx, ry, re, rz = bufs
         made = []
-        for i, (offset, what, at) in enumerate(messages):
+        for i, (offset, what, at, stage) in enumerate(messages):
             if what == "x":
                 src, dst = px.at[at[0]], rx.at[at[0], at[1]]
             elif what == "xz":
-                src, dst = pq.at[at[0]], rx.at[at[0], at[1]]
+                src, dst = pq.at[at[1], at[0]], rx.at[at[0], 3 + at[1]]
             elif what == "e":
-                src, dst = pe, re.at[at[0], at[1]]
+                src, dst = pe.at[at[1]], re.at[at[0], at[1]]
             elif what == "z":
-                src, dst = pz.at[at[0]], rz.at[at[0]]
-            elif what == "yy":
-                src, dst = py.at[here[1]], ry.at[here[1]]
+                part = pl.ds(5 * at[1], 5)
+                src, dst = pz.at[at[0], part], rz.at[at[0], part]
             else:
-                src, dst = py.at[at[0]], ry.at[at[0]]
-            made.append((offset, what in EARLY, pltpu.make_async_remote_copy(
+                part = pl.ds(face_rows(nz) * at[1], face_rows(nz))
+                way = here[1] if what == "yy" else at[0]
+                src, dst = py.at[way, part], ry.at[way, part]
+            made.append((offset, stage, pltpu.make_async_remote_copy(
                 src_ref=src, dst_ref=dst, send_sem=send.at[i], recv_sem=recv.at[i],
                 device_id=target(offset), device_id_type=MESH,
             )))
         return made
 
-    def start(made, early):
-        guarded([m for m in made if m[1] == early], 1, lambda m: m[2].start())
+    def start(made, stage):
+        guarded([m for m in made if m[1] == stage], 1, lambda m: m[2].start())
 
     def arrive(made):
         guarded(made, -1, lambda m: m[2].wait_recv())
@@ -387,14 +398,18 @@
     inlet_speed = 0.1 * (1.0 + 0.8 * jnp.sin(angle))
     zero = jnp.zeros((8, 128), jnp.float32)
 
-    sent1 = copies((px1, pq1, py1, pe1, pz1, rx1, ry1, re1, rz1), send1, recv1)
-    sent2 = copies((px2, pq2, py2, pe2, pz2, rx2, ry2, re2, rz2), send2, recv2)
-    loads[0].wait()
-    loads[1].wait()
+    sent1 = copies(both, (px1, pq1, py1, pe1, pz1, rx1, ry1, re1, rz1), send1, recv1)
+    sent2 = copies(alone, (px2, pq2, py2, pe2, pz2, rx2, ry2, re2, rz2), send2, recv2)
     for turn, z in enumerate(depth_order(nz)):
-        loads[2 + 2 * turn].wait()
+        loads[turn].wait()
         first.scatter(1, z, [adj[q, z] for q in range(Q)])
-        loads[3 + 2 * turn].wait()
+    pl.semaphore_wait(barrier, expected)
+    start(sent1, 0)
+
+    loads[nz].wait()
+    loads[nz + 1].wait()
+    for turn, z in enumerate(depth_order(nz)):
+        loads[nz + 2 + turn].wait()
         n = kind[z]
         fluid = n == 0
         inlet = n == 2
@@ -419,12 +434,11 @@
         saved[z, 4] = keep
         saved[z, 5] = jnp.where(fluid, k, 0.0)
         saved[z, 6] = -0.11 / (denom * denom)
-        if turn == 1:
-            first.pack(pq1)
-            pl.semaphore_wait(barrier, expected)
-            start(sent1, True)
+        if turn < 2:
+            first.pack(pq1, 1 - turn)
+            start(sent1, 1 + turn)
     first.pack(px1)
-    start(sent1, False)
+    start(sent1, 3)
     arrive(sent1)
 
     for turn, z in enumerate(depth_order(nz)):
@@ -434,11 +448,11 @@
             first.gather(1, z, merge), r, u, saved_cells(saved, kind, z))
         part[z] = by_damp
         second.scatter(0, z, a)
-        if turn == 1:
-            second.pack(pq2)
-            start(sent2, True)
+        if turn < 2:
+            second.pack(pq2, 1 - turn)
+            start(sent2, 1 + turn)
     second.pack(px2)
-    start(sent2, False)
+    start(sent2, 3)
     leave(sent1)
     arrive(sent2)
     leave(sent2)
@@ -472,14 +486,14 @@
 
 
 def packed_shapes(fields, nz):
-    rows = -(-fields * 5 * nz // 8) * 8
+    rows = fields * face_rows(nz)
     return [
-        (2, 8, 128), (2, 8, 128), (2, rows, 128), (8, 128), (2, fields * 5, 8, 128),
+        (2, 8, 128), (2, 2, 8, 128), (2, rows, 128), (2, 8, 128), (2, fields * 5, 8, 128),
     ]
 
 
 def landing_shapes(fields, nz):
-    rows = -(-fields * 5 * nz // 8) * 8
+    rows = fields * face_rows(nz)
     return [
         (fields, Q, nz, 8, 128), (2, 5, 8, 128), (2, rows, 128), (2, 2, 8, 128),
         (2, fields * 5, 8, 128),
@@ -495,7 +509,7 @@
     f32 = jnp.float32
     i32 = jnp.int32
     merge = sizes[1] == 2
-    count = len(message_list(merge))
+    counts = [len(message_list(merge, fields)) for fields in (2, 2, 1, 1)]
     any_space = pl.BlockSpec(memory_space=pl.ANY)
     vmem = pl.BlockSpec(memory_space=pltpu.VMEM)
     handed = [
@@ -515,7 +529,7 @@
             pltpu.VMEM(populations.shape, f32),
             pltpu.VMEM(porosity.shape, f32),
             pltpu.SemaphoreType.DMA((2 + 2 * nz,)),
-        ] + [pltpu.VMEM(s, f32) for s in scratch] + [pltpu.SemaphoreType.DMA((count,))] * 4,
+        ] + [pltpu.VMEM(s, f32) for s in scratch] + [pltpu.SemaphoreType.DMA((c,)) for c in counts],
         compiler_params=pltpu.CompilerParams(
             collective_id=0, has_side_effects=True, vmem_limit_bytes=LIMIT),
     )(step_index, *[

time: 15.2 us -> 15.1 us (level)
  no operation moved by 1% of the time
where the time goes in v4:
time: 15.1 us; the launch traced here: 14.9 us
  Pallas kernels  13.6 us (90%)
  between operations  1.28 us (8%)
    pallas_call x1, Pallas kernels, on_device(): pl.pallas_call(functools.partial(window, sizes, nz), out_shape=handed, in...  12.7 us
    pallas_call x1, Pallas kernels, on_device(): pl.pallas_call(functools.partial(last_step, merge, nz), out_shape=(jax.Sh...  0.9 us

profile of v4, /device:TPU:0, one launch (start us, length us, event | category | flops | bytes accessed | tf_op | source)
XLA Modules:
  0.0 14.9 jit_solution(7934645999817658810)
XLA Ops:
  1.3 12.7 %shard_map.68 = (f32[19,4,8,128]{3,2,1,0:T(8,128)S(1)}, s32[4,8,128]{2,1,0:T(8,128)S(1)}, f32[4,7,8,128]{3,2,1,0:T(8,128)S(1)}, f32[4,8,128]{2,1,0:T(8,128)S(1)}...) custom-call(s32[1]{0:T(128)S(6)} %copy.7.step, ...), custom_call_target="tpu_custom_call" | custom-call | tf_op jit(solution)/shard_map/pallas_call | solution.py:523
  14.0 0.9 %shard_map.69 = (f32[19,4,8,128]{3,2,1,0:T(8,128)}, f32[4,8,128]{2,1,0:T(8,128)}) custom-call(f32[19,4,8,128]{3,2,1,0:T(8,128)S(1)} %get-tuple-element.12.adj, s32[4,8,128]{2,1,0:T(8,128)S(1)} %get-tuple-element.13.kind, f32[4,7,8,128]{3,2,1,0:T(8,128)S(1)} %get-tuple-element.14.saved, f32[4,8,128]{2,1,0:T(8,128)S(1)} %get-tuple-element.15.part, ...), custom_call_target="tpu_custom_call" | custom-call | tf_op jit(solution)/shard_map/pallas_call | solution.py:539

commit v5 on v4

--- a/solution.py
+++ b/solution.py
@@ -56,31 +56,41 @@
     return place
 
 
-def message_list(merge, fields):
-    ys = (1,) if merge else SIGNS
-    out = []
-    for fi in reversed(range(fields)):
-        for oz in SIGNS:
-            stage = 0 if fi else 1 + (oz == 1)
-            out.append(((0, 0, oz), "z", (side(oz), fi), stage))
-        for oy in ys:
-            stage = 0 if fi else 3
-            out.append(((0, oy, 0), "yy" if merge else "y", (side(oy), fi), stage))
-    for oz in SIGNS:
-        stage = 1 + (oz == 1)
-        out += [((ox, 0, oz), "xz", (side(ox), side(oz)), stage) for ox in SIGNS]
-        out += [((0, oy, oz), "e", (side(oy), side(oz)), stage) for oy in ys]
-    for ox in SIGNS:
-        out += [((ox, oy, 0), "x", (side(ox), 1 + side(oy)), 3) for oy in ys]
-    out += [((ox, 0, 0), "x", (side(ox), 0), 3) for ox in SIGNS]
-    rank = {"xz": 0, "e": 1, "z": 2, "x": 3, "yy": 4, "y": 4}
-    last = {(0, 0): 5}
-    return sorted(out, key=lambda m: (
-        m[3], last.get(m[0][1:], rank[m[1]]) if m[1] == "x" else rank[m[1]]))
-
-
 def face_rows(nz):
     return -(-5 * nz // 8) * 8
+
+
+def bounded(offset, merge):
+    return (0 if merge else offset[1], offset[2])
+
+
+class Plan:
+    def __init__(self, merge, fields, nz):
+        ys = (1,) if merge else SIGNS
+        found = []
+        for oz in SIGNS:
+            stage = 1 + (oz == 1)
+            found += [((ox, 0, oz), "xz", (side(ox), side(oz)), stage, 1) for ox in SIGNS]
+            found += [((0, oy, oz), "e", (side(oy), side(oz)), stage, 1) for oy in ys]
+            found.append(((0, 0, oz), "z", (side(oz),), stage, 5 * fields))
+        for ox in SIGNS:
+            found += [((ox, oy, 0), "xy", (side(ox), side(oy)), 3, 1) for oy in ys]
+        for oy in ys:
+            found.append(((0, oy, 0), "y", (side(oy),), 3, fields * face_rows(nz) // 8))
+        found += [((ox, 0, 0), "x", (side(ox),), 3, 1) for ox in SIGNS]
+        self.merge = merge
+        self.groups = {}
+        for m in found:
+            self.groups.setdefault(bounded(m[0], merge), []).append(m)
+        self.pieces = {}
+        self.place = {}
+        self.tiles = 0
+        for steps, group in self.groups.items():
+            first = self.tiles
+            for m in group:
+                self.place[m[1], m[2]] = (self.tiles, m[4])
+                self.tiles += m[4]
+            self.pieces[steps] = (first, self.tiles - first)
 
 
 def total(items):
@@ -165,11 +175,12 @@
 
 
 class Exchange:
-    def __init__(self, signs, nz, refs):
+    def __init__(self, signs, nz, plan, refs):
         self.signs = signs
         self.nz = nz
         self.px, self.pq, self.py, self.pe, self.pz = refs[:5]
-        self.kept, self.rx, self.ry, self.re, self.rz = refs[5:]
+        self.kept, self.land = refs[5:]
+        self.plan = plan
         self.count = 5 * nz
         self.rows = face_rows(nz)
         self.lane = lax.broadcasted_iota(jnp.int32, (8, 128), 1)
@@ -214,42 +225,47 @@
                     self.pe[side(mz), e : e + 1, :] = edge
                 else:
                     k = fi * self.rows + place[1][q] * nz + zp
-                    self.py[s, k : k + 1, :] = edge
+                    self.py[s, k // 8, k % 8 : k % 8 + 1, :] = edge
 
     def pack(self, target, *at):
         for s in (0, 1):
             target[(*at, s)] = self.packed[s]
 
-    def gather(self, fi, z, merge, given=None):
+    def landed(self, what, *at):
+        if self.plan.merge and what in ("xy", "e", "y"):
+            at = {"xy": at[:1] + (0,), "e": (0,) + at[1:], "y": (0,)}[what]
+        return self.plan.place[what, at][0]
+
+    def gather(self, fi, z, given=None):
         nz = self.nz
+        land = self.land
         out = []
         for q in range(Q):
             mx, my, mz = self.moves[fi][q]
             place = self.places[fi]
             wraps = (mz == 1 and z == 0) or (mz == -1 and z == nz - 1)
             if wraps:
-                t = self.rz[side(mz), fi * 5 + place[2][q]]
+                t = land[self.landed("z", side(mz)) + fi * 5 + place[2][q]]
             else:
                 t = self.kept[fi, q, z]
-            sy = 0 if merge else side(my)
             w = 0 if my == 1 else 7
             if my:
                 if wraps:
                     e = self.edge_row(fi, my)
-                    edge = self.re[sy, side(mz), e : e + 1, :]
+                    edge = land[self.landed("e", side(my), side(mz)), e : e + 1, :]
                 else:
                     k = fi * self.rows + place[1][q] * nz + z
-                    edge = self.ry[side(my), k : k + 1, :]
+                    edge = land[self.landed("y", side(my)) + k // 8, k % 8 : k % 8 + 1, :]
                 t = jnp.where(self.row == w, jnp.broadcast_to(edge, (8, 128)), t)
             if mx:
                 s = side(mx)
                 k = fi * self.count + place[0][q] * nz + z
                 if wraps:
-                    col = self.rx[s, 3 + side(mz)]
+                    col = land[self.landed("xz", s, side(mz))]
                 else:
-                    col = self.rx[s, 0]
+                    col = land[self.landed("x", s)]
                     if my:
-                        col = jnp.where(self.row == w, self.rx[s, 1 + sy], col)
+                        col = jnp.where(self.row == w, land[self.landed("xy", s, side(my))], col)
                 target = 0 if mx == 1 else 127
                 shift = (target - k) % 128
                 if shift:
@@ -283,34 +299,22 @@
 def window(
     sizes, nz,
     step, pop_hbm, por_hbm, kind_hbm, adj_hbm,
-    adj, kind, saved, part, edges, kept2, rx2, ry2, re2, rz2,
+    adj, kind, saved, part, edges, kept2, land2,
     pop, por, load_sem,
     px1, pq1, py1, pe1, pz1, px2, pq2, py2, pe2, pz2,
-    kept1, rx1, ry1, re1, rz1,
+    kept1, land1,
     send1, recv1, send2, recv2,
 ):
     merge = sizes[1] == 2
     names = ("gx", "gy", "gz")
     here = [lax.axis_index(n) for n in names]
-    both, alone = message_list(merge, 2), message_list(merge, 1)
-
-    pairs = [(adj_hbm.at[:, z], adj.at[:, z]) for z in depth_order(nz)]
-    pairs += [(por_hbm, por), (kind_hbm, kind)]
-    pairs += [(pop_hbm.at[:, z], pop.at[:, z]) for z in depth_order(nz)]
-    loads = [
-        pltpu.make_async_copy(src, dst, load_sem.at[i]) for i, (src, dst) in enumerate(pairs)
-    ]
-    for c in loads:
-        c.start()
+    both, alone = Plan(merge, 2, nz), Plan(merge, 1, nz)
 
     def target(offset):
         return {
             n: lax.rem(here[d] + (offset[d] + sizes[d]), sizes[d])
             for d, n in enumerate(names) if offset[d]
         }
-
-    def bounded(offset):
-        return (0 if merge else offset[1], offset[2])
 
     def inside(steps, way):
         ok = None
@@ -321,62 +325,64 @@
                 ok = test if ok is None else jnp.logical_and(ok, test)
         return ok
 
-    def guarded(items, way, act):
-        groups = {}
-        for item in items:
-            groups.setdefault(bounded(item[0]), []).append(item)
-        for steps, group in groups.items():
-            def every(group=group):
-                for item in group:
-                    act(item)
-            ok = inside(steps, way)
-            if ok is None:
-                every()
-            else:
-                pl.when(ok)(every)
+    def guarded(steps, way, act):
+        ok = inside(steps, way)
+        if ok is None:
+            act()
+        else:
+            pl.when(ok)(act)
 
     barrier = pltpu.get_barrier_semaphore()
-    guarded(alone, 1, lambda m: pl.semaphore_signal(
-        barrier, inc=1, device_id=target(m[0]), device_id_type=MESH))
     expected = 0
-    for offset, _, _, _ in alone:
-        ok = inside(bounded(offset), -1)
-        expected = expected + (1 if ok is None else jnp.where(ok, 1, 0))
-
-    def copies(messages, bufs, send, recv):
-        px, pq, py, pe, pz, rx, ry, re, rz = bufs
-        made = []
-        for i, (offset, what, at, stage) in enumerate(messages):
-            if what == "x":
-                src, dst = px.at[at[0]], rx.at[at[0], at[1]]
-            elif what == "xz":
-                src, dst = pq.at[at[1], at[0]], rx.at[at[0], 3 + at[1]]
-            elif what == "e":
-                src, dst = pe.at[at[1]], re.at[at[0], at[1]]
-            elif what == "z":
-                part = pl.ds(5 * at[1], 5)
-                src, dst = pz.at[at[0], part], rz.at[at[0], part]
-            else:
-                part = pl.ds(face_rows(nz) * at[1], face_rows(nz))
-                way = here[1] if what == "yy" else at[0]
-                src, dst = py.at[way, part], ry.at[way, part]
-            made.append((offset, stage, pltpu.make_async_remote_copy(
-                src_ref=src, dst_ref=dst, send_sem=send.at[i], recv_sem=recv.at[i],
-                device_id=target(offset), device_id_type=MESH,
-            )))
-        return made
-
-    def start(made, stage):
-        guarded([m for m in made if m[1] == stage], 1, lambda m: m[2].start())
-
-    def arrive(made):
-        guarded(made, -1, lambda m: m[2].wait_recv())
-
-    def leave(made):
-        guarded(made, 1, lambda m: m[2].wait_send())
-
-    first = Exchange((1, -1), nz, (px1, pq1, py1, pe1, pz1, kept1, rx1, ry1, re1, rz1))
-    second = Exchange((-1,), nz, (px2, pq2, py2, pe2, pz2, kept2, rx2, ry2, re2, rz2))
+    for steps, group in alone.groups.items():
+        def greet(group=group):
+            for m in group:
+                pl.semaphore_signal(
+                    barrier, inc=1, device_id=target(m[0]), device_id_type=MESH)
+        guarded(steps, 1, greet)
+        ok = inside(steps, -1)
+        expected = expected + (len(group) if ok is None else jnp.where(ok, len(group), 0))
+
+    pairs = [(pop_hbm, pop), (adj_hbm, adj), (por_hbm, por), (kind_hbm, kind)]
+    loads = [
+        pltpu.make_async_copy(src, dst, load_sem.at[i]) for i, (src, dst) in enumerate(pairs)
+    ]
+    for c in loads:
+        c.start()
+
+    def source(what, at, bufs):
+        px, pq, py, pe, pz = bufs
+        if what in ("x", "xy"):
+            return px.at[pl.ds(at[0], 1)]
+        if what == "xz":
+            return pq.at[at[1], pl.ds(at[0], 1)]
+        if what == "e":
+            return pe.at[pl.ds(at[1], 1)]
+        if what == "z":
+            return pz.at[at[0]]
+        return py.at[here[1] if merge else at[0]]
+
+    def start(plan, bufs, land, sems, stages):
+        for i, (steps, group) in enumerate(plan.groups.items()):
+            chosen = [m for m in group if m[3] in stages]
+            def send(i=i, chosen=chosen):
+                for offset, what, at, _, _ in chosen:
+                    pltpu.make_async_remote_copy(
+                        src_ref=source(what, at, bufs),
+                        dst_ref=land.at[pl.ds(*plan.place[what, at])],
+                        send_sem=sems[0].at[i], recv_sem=sems[1].at[i],
+                        device_id=target(offset), device_id_type=MESH,
+                    ).start()
+            if chosen:
+                guarded(steps, 1, send)
+
+    def settle(plan, land, sem, way):
+        for i, (steps, piece) in enumerate(plan.pieces.items()):
+            whole = land.at[pl.ds(*piece)]
+            guarded(steps, way, pltpu.make_async_copy(whole, whole, sem.at[i]).wait)
+
+    first = Exchange((1, -1), nz, both, (px1, pq1, py1, pe1, pz1, kept1, land1))
+    second = Exchange((-1,), nz, alone, (px2, pq2, py2, pe2, pz2, kept2, land2))
 
     pe1[...] = jnp.zeros_like(pe1)
     py1[...] = jnp.zeros_like(py1)
@@ -398,18 +404,12 @@
     inlet_speed = 0.1 * (1.0 + 0.8 * jnp.sin(angle))
     zero = jnp.zeros((8, 128), jnp.float32)
 
-    sent1 = copies(both, (px1, pq1, py1, pe1, pz1, rx1, ry1, re1, rz1), send1, recv1)
-    sent2 = copies(alone, (px2, pq2, py2, pe2, pz2, rx2, ry2, re2, rz2), send2, recv2)
+    packs1 = (px1, pq1, py1, pe1, pz1)
+    packs2 = (px2, pq2, py2, pe2, pz2)
+    for c in loads:
+        c.wait()
     for turn, z in enumerate(depth_order(nz)):
-        loads[turn].wait()
         first.scatter(1, z, [adj[q, z] for q in range(Q)])
-    pl.semaphore_wait(barrier, expected)
-    start(sent1, 0)
-
-    loads[nz].wait()
-    loads[nz + 1].wait()
-    for turn, z in enumerate(depth_order(nz)):
-        loads[nz + 2 + turn].wait()
         n = kind[z]
         fluid = n == 0
         inlet = n == 2
@@ -436,40 +436,40 @@
         saved[z, 6] = -0.11 / (denom * denom)
         if turn < 2:
             first.pack(pq1, 1 - turn)
-            start(sent1, 1 + turn)
     first.pack(px1)
-    start(sent1, 3)
-    arrive(sent1)
+    pl.semaphore_wait(barrier, expected)
+    start(both, packs1, land1, (send1, recv1), (1, 2, 3))
+    settle(both, land1, recv1, -1)
 
     for turn, z in enumerate(depth_order(nz)):
-        r, flow = first_moments(first.gather(0, z, merge))
+        r, flow = first_moments(first.gather(0, z))
         u = [m / r for m in flow]
         a, by_damp = pulled_back(
-            first.gather(1, z, merge), r, u, saved_cells(saved, kind, z))
+            first.gather(1, z), r, u, saved_cells(saved, kind, z))
         part[z] = by_damp
         second.scatter(0, z, a)
         if turn < 2:
             second.pack(pq2, 1 - turn)
-            start(sent2, 1 + turn)
+            start(alone, packs2, land2, (send2, recv2), (1 + turn,))
     second.pack(px2)
-    start(sent2, 3)
-    leave(sent1)
-    arrive(sent2)
-    leave(sent2)
+    start(alone, packs2, land2, (send2, recv2), (3,))
+    settle(both, land1, send1, 1)
+    settle(alone, land2, recv2, -1)
+    settle(alone, land2, send2, 1)
 
 
 def last_step(
     merge, nz,
-    adj, kind, saved, part, edges, kept, rx, ry, re, rz,
+    adj, kind, saved, part, edges, kept, land,
     out_hbm, sens_hbm,
     out, sens, out_sem, sens_sem,
 ):
-    field = Exchange((-1,), nz, (None,) * 5 + (kept, rx, ry, re, rz))
+    field = Exchange((-1,), nz, Plan(merge, 1, nz), (None,) * 5 + (kept, land))
     span = edges[0] == 1
     depth = (edges[1] == 1, edges[2] == 1)
     copies = []
     for z in range(nz):
-        g = field.gather(0, z, merge, (span, depth, lambda q, z=z: adj[q, z]))
+        g = field.gather(0, z, (span, depth, lambda q, z=z: adj[q, z]))
         u = [saved[z, 1 + d] for d in range(3)]
         a, by_damp = pulled_back(g, saved[z, 0], u, saved_cells(saved, kind, z))
         sens[z] = jnp.where(kind[z] == 0, saved[z, 6] * (part[z] + by_damp), 0.0)
@@ -486,18 +486,14 @@
 
 
 def packed_shapes(fields, nz):
-    rows = fields * face_rows(nz)
     return [
-        (2, 8, 128), (2, 2, 8, 128), (2, rows, 128), (2, 8, 128), (2, fields * 5, 8, 128),
+        (2, 8, 128), (2, 2, 8, 128), (2, fields * face_rows(nz) // 8, 8, 128),
+        (2, 8, 128), (2, fields * 5, 8, 128),
     ]
 
 
-def landing_shapes(fields, nz):
-    rows = fields * face_rows(nz)
-    return [
-        (fields, Q, nz, 8, 128), (2, 5, 8, 128), (2, rows, 128), (2, 2, 8, 128),
-        (2, fields * 5, 8, 128),
-    ]
+def landing_shapes(plan, fields, nz):
+    return [(fields, Q, nz, 8, 128), (plan.tiles, 8, 128)]
 
 
 LIMIT = 8 * 1024 * 1024
@@ -509,7 +505,8 @@
     f32 = jnp.float32
     i32 = jnp.int32
     merge = sizes[1] == 2
-    counts = [len(message_list(merge, fields)) for fields in (2, 2, 1, 1)]
+    both, alone = Plan(merge, 2, nz), Plan(merge, 1, nz)
+    groups = pltpu.SemaphoreType.DMA((len(both.groups),))
     any_space = pl.BlockSpec(memory_space=pl.ANY)
     vmem = pl.BlockSpec(memory_space=pltpu.VMEM)
     handed = [
@@ -518,8 +515,8 @@
         pltpu.VMEM((nz, 7, 8, 128), f32),
         pltpu.VMEM(porosity.shape, f32),
         pltpu.VMEM((3, 8, 128), i32),
-    ] + [pltpu.VMEM(s, f32) for s in landing_shapes(1, nz)]
-    scratch = packed_shapes(2, nz) + packed_shapes(1, nz) + landing_shapes(2, nz)
+    ] + [pltpu.VMEM(s, f32) for s in landing_shapes(alone, 1, nz)]
+    scratch = packed_shapes(2, nz) + packed_shapes(1, nz) + landing_shapes(both, 2, nz)
     state = pl.pallas_call(
         functools.partial(window, sizes, nz),
         out_shape=handed,
@@ -528,8 +525,8 @@
         scratch_shapes=[
             pltpu.VMEM(populations.shape, f32),
             pltpu.VMEM(porosity.shape, f32),
-            pltpu.SemaphoreType.DMA((2 + 2 * nz,)),
-        ] + [pltpu.VMEM(s, f32) for s in scratch] + [pltpu.SemaphoreType.DMA((c,)) for c in counts],
+            pltpu.SemaphoreType.DMA((4,)),
+        ] + [pltpu.VMEM(s, f32) for s in scratch] + [groups] * 4,
         compiler_params=pltpu.CompilerParams(
             collective_id=0, has_side_effects=True, vmem_limit_bytes=LIMIT),
     )(step_index, *[

time: 15.1 us -> 14.6 us (0.967)
  Pallas kernels: 13.6 us -> 13.1 us
    pallas_call x1, Pallas kernels: 12.7 us -> 12.2 us  [on_device(): pl.pallas_call(functools.partial(window, sizes, nz), out_shape=handed, in...]
where the time goes in v5:
time: 14.6 us; the launch traced here: 14.4 us
  Pallas kernels  13.1 us (90%)
  between operations  1.28 us (9%)
    pallas_call x1, Pallas kernels, on_device(): pl.pallas_call(functools.partial(window, sizes, nz), out_shape=handed, in...  12.2 us
    pallas_call x1, Pallas kernels, on_device(): pl.pallas_call(functools.partial(last_step, merge, nz), out_shape=(jax.Sh...  0.9 us

profile of v5, /device:TPU:0, one launch (start us, length us, event | category | flops | bytes accessed | tf_op | source)
XLA Modules:
  0.0 14.4 jit_solution(11434042792656997247)
XLA Ops:
  1.3 12.2 %shard_map.68 = (f32[19,4,8,128]{3,2,1,0:T(8,128)S(1)}, s32[4,8,128]{2,1,0:T(8,128)S(1)}, f32[4,7,8,128]{3,2,1,0:T(8,128)S(1)}, f32[4,8,128]{2,1,0:T(8,128)S(1)}...) custom-call(s32[1]{0:T(128)S(6)} %copy.7.step, ...), custom_call_target="tpu_custom_call" | custom-call | tf_op jit(solution)/shard_map/pallas_call | solution.py:520
  13.5 0.9 %shard_map.69 = (f32[19,4,8,128]{3,2,1,0:T(8,128)}, f32[4,8,128]{2,1,0:T(8,128)}) custom-call(f32[19,4,8,128]{3,2,1,0:T(8,128)S(1)} %get-tuple-element.9.adj, s32[4,8,128]{2,1,0:T(8,128)S(1)} %get-tuple-element.10.kind, f32[4,7,8,128]{3,2,1,0:T(8,128)S(1)} %get-tuple-element.11.saved, f32[4,8,128]{2,1,0:T(8,128)S(1)} %get-tuple-element.12.part, ...), custom_call_target="tpu_custom_call" | custom-call | tf_op jit(solution)/shard_map/pallas_call | solution.py:536

commit v6 on v5

--- a/solution.py
+++ b/solution.py
@@ -310,6 +310,13 @@
     here = [lax.axis_index(n) for n in names]
     both, alone = Plan(merge, 2, nz), Plan(merge, 1, nz)
 
+    pairs = [(adj_hbm, adj), (pop_hbm, pop), (por_hbm, por), (kind_hbm, kind)]
+    loads = [
+        pltpu.make_async_copy(src, dst, load_sem.at[i]) for i, (src, dst) in enumerate(pairs)
+    ]
+    for c in loads:
+        c.start()
+
     def target(offset):
         return {
             n: lax.rem(here[d] + (offset[d] + sizes[d]), sizes[d])
@@ -342,13 +349,6 @@
         guarded(steps, 1, greet)
         ok = inside(steps, -1)
         expected = expected + (len(group) if ok is None else jnp.where(ok, len(group), 0))
-
-    pairs = [(pop_hbm, pop), (adj_hbm, adj), (por_hbm, por), (kind_hbm, kind)]
-    loads = [
-        pltpu.make_async_copy(src, dst, load_sem.at[i]) for i, (src, dst) in enumerate(pairs)
-    ]
-    for c in loads:
-        c.start()
 
     def source(what, at, bufs):
         px, pq, py, pe, pz = bufs
@@ -406,10 +406,12 @@
 
     packs1 = (px1, pq1, py1, pe1, pz1)
     packs2 = (px2, pq2, py2, pe2, pz2)
-    for c in loads:
+    loads[0].wait()
+    for z in range(nz):
+        first.scatter(1, z, [adj[q, z] for q in range(Q)])
+    for c in loads[1:]:
         c.wait()
     for turn, z in enumerate(depth_order(nz)):
-        first.scatter(1, z, [adj[q, z] for q in range(Q)])
         n = kind[z]
         fluid = n == 0
         inlet = n == 2

time: 14.6 us -> 14.6 us (level)
  no operation moved by 1% of the time
where the time goes in v6:
time: 14.6 us; the launch traced here: 14.4 us
  Pallas kernels  13.1 us (90%)
  between operations  1.28 us (9%)
    pallas_call x1, Pallas kernels, on_device(): pl.pallas_call(functools.partial(window, sizes, nz), out_shape=handed, in...  12.2 us
    pallas_call x1, Pallas kernels, on_device(): pl.pallas_call(functools.partial(last_step, merge, nz), out_shape=(jax.Sh...  0.9 us

profile of v6, /device:TPU:0, one launch (start us, length us, event | category | flops | bytes accessed | tf_op | source)
XLA Modules:
  0.0 14.4 jit_solution(5411276434027068546)
XLA Ops:
  1.3 12.2 %shard_map.68 = (f32[19,4,8,128]{3,2,1,0:T(8,128)S(1)}, s32[4,8,128]{2,1,0:T(8,128)S(1)}, f32[4,7,8,128]{3,2,1,0:T(8,128)S(1)}, f32[4,8,128]{2,1,0:T(8,128)S(1)}...) custom-call(s32[1]{0:T(128)S(6)} %copy.7.step, ...), custom_call_target="tpu_custom_call" | custom-call | tf_op jit(solution)/shard_map/pallas_call | solution.py:522
  13.5 0.9 %shard_map.69 = (f32[19,4,8,128]{3,2,1,0:T(8,128)}, f32[4,8,128]{2,1,0:T(8,128)}) custom-call(f32[19,4,8,128]{3,2,1,0:T(8,128)S(1)} %get-tuple-element.9.adj, s32[4,8,128]{2,1,0:T(8,128)S(1)} %get-tuple-element.10.kind, f32[4,7,8,128]{3,2,1,0:T(8,128)S(1)} %get-tuple-element.11.saved, f32[4,8,128]{2,1,0:T(8,128)S(1)} %get-tuple-element.12.part, ...), custom_call_target="tpu_custom_call" | custom-call | tf_op jit(solution)/shard_map/pallas_call | solution.py:538

commit v7 on v5

--- a/solution.py
+++ b/solution.py
@@ -362,9 +362,9 @@
             return pz.at[at[0]]
         return py.at[here[1] if merge else at[0]]
 
-    def start(plan, bufs, land, sems, stages):
+    def start(plan, bufs, land, sems, stages, skip=()):
         for i, (steps, group) in enumerate(plan.groups.items()):
-            chosen = [m for m in group if m[3] in stages]
+            chosen = [m for m in group if m[3] in stages and m[1] not in skip]
             def send(i=i, chosen=chosen):
                 for offset, what, at, _, _ in chosen:
                     pltpu.make_async_remote_copy(
@@ -438,7 +438,9 @@
             first.pack(pq1, 1 - turn)
     first.pack(px1)
     pl.semaphore_wait(barrier, expected)
-    start(both, packs1, land1, (send1, recv1), (1, 2, 3))
+    start(both, packs1, land1, (send1, recv1), (3,), ("x", "y"))
+    start(both, packs1, land1, (send1, recv1), (1, 2))
+    start(both, packs1, land1, (send1, recv1), (3,), ("xy",))
     settle(both, land1, recv1, -1)
 
     for turn, z in enumerate(depth_order(nz)):

time: 14.6 us -> 14.6 us (level)
  no operation moved by 1% of the time
where the time goes in v7:
time: 14.6 us; the launch traced here: 14.4 us
  Pallas kernels  13.1 us (90%)
  between operations  1.28 us (9%)
    pallas_call x1, Pallas kernels, on_device(): pl.pallas_call(functools.partial(window, sizes, nz), out_shape=handed, in...  12.2 us
    pallas_call x1, Pallas kernels, on_device(): pl.pallas_call(functools.partial(last_step, merge, nz), out_shape=(jax.Sh...  0.9 us

profile of v7, /device:TPU:0, one launch (start us, length us, event | category | flops | bytes accessed | tf_op | source)
XLA Modules:
  0.0 14.4 jit_solution(13428815047035855247)
XLA Ops:
  1.3 12.2 %shard_map.68 = (f32[19,4,8,128]{3,2,1,0:T(8,128)S(1)}, s32[4,8,128]{2,1,0:T(8,128)S(1)}, f32[4,7,8,128]{3,2,1,0:T(8,128)S(1)}, f32[4,8,128]{2,1,0:T(8,128)S(1)}...) custom-call(s32[1]{0:T(128)S(6)} %copy.7.step, ...), custom_call_target="tpu_custom_call" | custom-call | tf_op jit(solution)/shard_map/pallas_call | solution.py:522
  13.5 0.9 %shard_map.69 = (f32[19,4,8,128]{3,2,1,0:T(8,128)}, f32[4,8,128]{2,1,0:T(8,128)}) custom-call(f32[19,4,8,128]{3,2,1,0:T(8,128)S(1)} %get-tuple-element.9.adj, s32[4,8,128]{2,1,0:T(8,128)S(1)} %get-tuple-element.10.kind, f32[4,7,8,128]{3,2,1,0:T(8,128)S(1)} %get-tuple-element.11.saved, f32[4,8,128]{2,1,0:T(8,128)S(1)} %get-tuple-element.12.part, ...), custom_call_target="tpu_custom_call" | custom-call | tf_op jit(solution)/shard_map/pallas_call | solution.py:538
